TPU v7x, 512 devices: a whole 4x4x16 slice. The times are simulated.
512 devices in a mesh: img: 32 (over x, z_hi, core), ref: 16 (over y, z_lo).
Axes of the slice: x: 4, y: 4, z: 16 (z_hi: 4, z_lo: 4; z = z_hi * 4 + z_lo), core: 2. Of those that a mesh axis runs over, the one named last changes fastest.
Arguments:
- images: bfloat16 [2048, 2, 4224], P('img', None, 'ref'), may hold values from -40 to 40
- projections: bfloat16 [768, 2, 4224], P('ref'), may hold values from -3 to 3
- contrast_curve: float32 [16, 4224], replicated, may hold values from 0.2 to 1
- noise_weight: float32 [4224], replicated, may hold values from 0.5 to 2
- defocus_group: int32 [2048], P('img'), may hold values from 0 to 15
- shifts: int32 [9, 2], replicated, may hold values from -3 to 3, as said below
- orient_index: int32 [768], P('ref'), may hold values from 0 to 255
- orient_prior: float32 [256], replicated, may hold values from -1.4 to 1.4
Outputs:
- class_sums: float32 [768, 2, 4224], P('ref', None, 'img')
- contrast_weight: float32 [768, 4224], P('ref', 'img')
- evidence: float32 [2048], P('img')
Inputs may be any that keep to these rules, and one draw needn't show every extreme that they name: `shifts`: shift 0 is (0, 0); shift 1 moves 3 pixels along x and shift 2 moves -3 pixels along x.
All inputs are finite; a program needn't handle non-finite values.
Results may differ from a plain program's by a relative error of at most 0.0044.
Values may be sent and summed in bfloat16 or wider, within the bound.
A program may use at most 64 MiB of HBM per device.

v0:
```python
import math

import jax
import jax.numpy as jnp
from jax import lax
from jax.sharding import PartitionSpec as P

NPIX = 4224
BOX = 128
NSHIFT = 9


def phase_tables(shifts, pixel_count):
    pixel_index = lax.iota(jnp.int32, pixel_count)
    half_box = BOX // 2
    freq_x = (pixel_index % half_box).astype(jnp.float32)
    freq_y = (pixel_index // half_box - NPIX // BOX).astype(jnp.float32)
    move_x = shifts[:, 0].astype(jnp.float32)[:, None]
    move_y = shifts[:, 1].astype(jnp.float32)[:, None]
    phase_angle = 2.0 * math.pi / BOX * (move_x * freq_x[None, :] + move_y * freq_y[None, :])
    return (jnp.cos(phase_angle), jnp.sin(phase_angle))


def shifted(weighted, cosine_row, sine_row):
    real_part = weighted[:, 0, :].astype(jnp.float32)
    imag_part = weighted[:, 1, :].astype(jnp.float32)
    return jnp.stack(
        [
            real_part * cosine_row + imag_part * sine_row,
            imag_part * cosine_row - real_part * sine_row,
        ],
        axis=1,
    ).astype(jnp.bfloat16)


def on_device(
    images,
    projections,
    contrast_curve,
    noise_weight,
    defocus_group,
    shifts,
    orient_index,
    orient_prior,
):
    gathered = lax.all_gather(images, "ref", axis=2, tiled=True)
    image_count = gathered.shape[0]
    pixel_count = gathered.shape[2]
    proj_count = projections.shape[0]
    group_count = contrast_curve.shape[0]
    slice_width = pixel_count // lax.axis_size("img")
    members = (defocus_group[:, None] == lax.iota(jnp.int32, group_count)[None, :]).astype(
        jnp.float32
    )
    curve_rows = jnp.dot(members, contrast_curve, precision=lax.Precision.HIGHEST)
    gain_rows = curve_rows * noise_weight[None, :]
    weighted = (gathered.astype(jnp.float32) * gain_rows[:, None, :]).astype(jnp.bfloat16)
    cosine_table, sine_table = phase_tables(shifts, pixel_count)
    flat_proj = projections.reshape(proj_count, 2 * pixel_count)
    proj_wide = projections.astype(jnp.float32)
    proj_power = proj_wide[:, 0, :] * proj_wide[:, 0, :] + proj_wide[:, 1, :] * proj_wide[:, 1, :]
    power_gain = contrast_curve * contrast_curve * noise_weight[None, :]
    group_norm = jnp.einsum(
        "gk,jk->gj", 0.5 * power_gain, proj_power, precision=lax.Precision.HIGHEST
    )
    penalty = jnp.dot(members, group_norm, precision=lax.Precision.HIGHEST)
    orient_hits = (
        orient_index[:, None] == lax.iota(jnp.int32, orient_prior.shape[0])[None, :]
    ).astype(jnp.float32)
    orient_term = jnp.dot(orient_hits, orient_prior, precision=lax.Precision.HIGHEST)
    score_base = orient_term[None, :] - penalty
    score_list = []
    for shift_slot in range(NSHIFT):
        shift_layer = shifted(weighted, cosine_table[shift_slot], sine_table[shift_slot]).reshape(
            image_count, 2 * pixel_count
        )
        score_list.append(
            jnp.einsum("ik,jk->ij", shift_layer, flat_proj, preferred_element_type=jnp.float32)
            + score_base
        )
    scores = jnp.stack(score_list)
    local_high = jnp.max(scores, axis=(0, 2))
    highest = lax.pmax(local_high, "ref")
    totals = lax.psum(jnp.sum(jnp.exp(scores - highest[None, :, None]), axis=(0, 2)), "ref")
    evidence = highest + jnp.log(totals)
    weights = jnp.exp(scores - evidence[None, :, None]).astype(jnp.bfloat16)
    partial_value = jnp.zeros((proj_count, 2 * pixel_count), jnp.float32)
    for shift_slot in range(NSHIFT):
        shift_layer = shifted(weighted, cosine_table[shift_slot], sine_table[shift_slot]).reshape(
            image_count, 2 * pixel_count
        )
        partial_value = partial_value + jnp.einsum(
            "ij,ik->jk", weights[shift_slot], shift_layer, preferred_element_type=jnp.float32
        )
    class_sums = lax.psum_scatter(
        partial_value.reshape(proj_count, 2, pixel_count), "img", scatter_dimension=2, tiled=True
    )
    summed = jnp.sum(weights.astype(jnp.float32), axis=0)
    per_group = jnp.einsum("ij,ig->jg", summed, members, precision=lax.Precision.HIGHEST)
    per_group = lax.psum(per_group, "img")
    gain_slice = lax.dynamic_slice_in_dim(
        power_gain, lax.axis_index("img") * slice_width, slice_width, 1
    )
    contrast_weight = jnp.dot(per_group, gain_slice, precision=lax.Precision.HIGHEST)
    return (class_sums, contrast_weight, evidence)


def solution(mesh):
    in_specs = (P("img", None, "ref"), P("ref", None, None), P(), P(), P("img"), P(), P("ref"), P())
    out_specs = (P("ref", None, "img"), P("ref", "img"), P("img"))
    return jax.shard_map(
        on_device, mesh=mesh, in_specs=in_specs, out_specs=out_specs, check_vma=False
    )
```

profile of v0, /device:TPU:1, one launch (start us, length us, event | category | flops | bytes accessed | tf_op | source)
XLA Modules:
  0.0 590.9 jit_solution(13550643330395088067)
XLA Ops:
  7.3 1.8 copy.41
  10.9 1.4 slice_reduce_fusion
  14.5 84.6 %all-gather.2.cloned.1.call-done = bf16[64,2,4224]{0,1,2:T(2,128)(2,1)} async-done(((bf16[64,2,264]{0,1,2:T(2,128)(2,1)}), bf16[64,2,4224]{0,1,2:T(2,128)(2,1)}) %all-gather.2.cloned.1.call-update) | async-done | bytes 1081360 | tf_op jit(solution)/shard_map/all_gather | solution.py:46
  99.0 4.8 copy.42
  112.6 1.1 fusion.53
  122.2 1.1 fusion.49
  126.7 1.3 reduce_max.62
  127.9 1.3 reduce_max.57
  129.3 1.3 reduce_max.55
  130.6 1.3 reduce_max.53
  131.9 1.3 reduce_max.48
  134.4 35.6 %pmax.7 = f32[64]{0:T(128)S(1)} all-reduce(f32[64]{0:T(128)S(1)} %maximum_maximum_fusion), channel_id=1, replica_groups=mesh['img'=32,'ref'=16] {'ref'}, use_global_device_ids=true, to_apply=%region_9.10 | all-reduce | flops 64 | bytes 512 | tf_op jit(solution)/shard_map/pmax | solution.py:83
  171.0 31.5 %psum.14 = f32[64]{0:T(128)S(1)} all-reduce(f32[64]{0:T(128)S(1)} %exponential_reduce_fusion), channel_id=1, replica_groups=mesh['img'=32,'ref'=16] {'ref'}, use_global_device_ids=true, to_apply=%region_11.12 | all-reduce | flops 64 | bytes 512 | tf_op jit(solution)/shard_map/psum | solution.py:84
  203.8 1.1 copy-done.1
  205.1 1.2 copy-done.2
  206.3 1.2 copy-done.3
  207.5 1.2 copy-done.4
  208.8 1.2 copy-done.5
  210.0 1.2 copy-done.6
  214.5 2.2 reshape.351
  216.7 1.3 dynamic-slice
  218.9 110.0 %psum.15 = f32[48,16]{0,1:T(8,128)S(1)} all-reduce(f32[48,16]{0,1:T(8,128)S(1)} %fusion.62), channel_id=1, replica_groups=mesh['img'=32,'ref'=16] {'img'}, use_global_device_ids=true, to_apply=%region_14.15 | all-reduce | flops 768 | bytes 6144 | tf_op jit(solution)/shard_map/psum | solution.py:100
  329.7 252.6 %all-reduce.3.cloned.1.call-done = f32[48,2,4224]{2,1,0:T(2,128)} async-done(((f32[48,2,4224]{2,1,0:T(2,128)}), f32[48,2,4224]{2,1,0:T(2,128)}) %all-reduce.3.cloned.1.call-update) | async-done | bytes 1622032
  582.4 1.7 constant_dynamic-slice_fusion
  (114 shorter events, 32.7 us)
Async XLA Ops:
  7.2 5.2 copy-start
  7.2 5.1 copy-start.7
  7.2 5.1 copy-start.10
  7.2 5.2 copy-start.26
  7.2 91.8 %all-gather.2.cloned.1.call-start = ((), (), s32[]{:S(2)}) async-start(), calls=%async_computation | async-start | bytes 2297856 | tf_op jit(solution)/shard_map/all_gather | solution.py:46
  9.0 3.5 copy-start.8
  9.0 573.3 %all-reduce.3.cloned.1.call-start = ((), (), s32[]{:S(2)}) async-start(), calls=%async_computation.1 | async-start | bytes 3244032
  13.8 92.4 %copy-start.27 = (f32[64,48]{0,1:T(8,128)}, f32[64,48]{0,1:T(8,128)S(1)}, u32[]{:S(2)}) copy-start(f32[64,48]{0,1:T(8,128)S(1)} %convolution_subtract_fusion) | copy-start | bytes 36868
  107.3 1.1 copy-start.9
  107.3 1.1 copy-start.28
  108.4 1.1 copy-start.16
  108.4 1.1 copy-start.17
  108.4 1.1 copy-start.18
  108.4 1.1 copy-start.19
  108.5 1.1 copy-start.20
  108.5 1.1 copy-start.21
  123.3 9.9 %copy-start.22 = (f32[64,48]{0,1:T(8,128)S(1)}, f32[64,48]{0,1:T(8,128)}, u32[]{:S(2)}) copy-start(f32[64,48]{0,1:T(8,128)} %get-tuple-element.58) | copy-start | bytes 36868
  203.7 1.2 copy-start.1
  205.0 1.2 copy-start.2
  206.2 1.2 copy-start.3
  207.5 1.2 copy-start.4
  208.7 1.2 copy-start.5
  209.9 1.2 copy-start.6
  216.6 2.0 copy-start.24
  (7 other events, 7.3 us)
Sparse Core Ops, SparseCore 0:
  10.1 88.8 all-gather.1
  216.8 365.5 all-reduce.2
where the time goes:
time: 592 us; the launch traced here: 591 us
  waiting for transfers between devices  337 us (57%)
  blocking collectives  177 us (30%)
  other arithmetic  23.9 us (4%)
  local copies, waits for them, and re-layouts  21.8 us (4%)
  matrix products  15.7 us (3%)
  between operations  15.1 us (3%)
    unnamed x3, waiting for transfers between devices  253 us
    psum x1, blocking collectives, on_device(): per_group = lax.psum(per_group, 'img')  110 us
    all_gather x1, waiting for transfers between devices, on_device(): gathered = lax.all_gather(images, 'ref', axis=2, tiled=True)  84.6 us
    pmax x1, blocking collectives, on_device(): highest = lax.pmax(local_high, 'ref')  35.6 us
    psum x1, blocking collectives, on_device(): lax.psum(jnp.sum(jnp.exp(scores - highest[None, :, None]), axis=(0, 2)),...  31.5 us
    unnamed x61, local copies, waits for them, and re-layouts  12.8 us
  transfers between devices with their start and end apart: 2, of which 2 were waited for; matrix products, arithmetic and copies ran while one was open for 1% of the time, Pallas kernels for 0%

commit v1 on v0

v1 whole, which is shorter than its diff:
```python
import math

import jax
import jax.numpy as jnp
from jax import lax
from jax.experimental import pallas as pl
from jax.experimental.pallas import tpu as pltpu
from jax.sharding import PartitionSpec as P

MESH = pl.DeviceIdType.MESH
F32 = jnp.float32
BF16 = jnp.bfloat16
HIGHEST = lax.Precision.HIGHEST
NT = (((1,), (1,)), ((), ()))
TN = (((0,), (0,)), ((), ()))

NPIX = 4224
BOX = 128
NSHIFT = 9
NIMG = 64
NPROJ = 48
GROUPS = 16
ROWS = NSHIFT * NIMG
SHARD = 272
PIECE = 48
MSG = 400
HALF = 208
FIRST = 112


def sincos(steps):
    quadrant = lax.shift_right_arithmetic(steps + 16, 5)
    rest = (steps - quadrant * 32).astype(F32) * (2.0 * math.pi / BOX)
    sq = rest * rest
    sin_part = rest * (
        1.0 + sq * (-1.0 / 6 + sq * (1.0 / 120 + sq * (-1.0 / 5040 + sq * (1.0 / 362880))))
    )
    cos_part = 1.0 + sq * (
        -0.5 + sq * (1.0 / 24 + sq * (-1.0 / 720 + sq * (1.0 / 40320 - sq * (1.0 / 3628800))))
    )
    odd = (quadrant & 1) == 1
    flip_sin = (quadrant & 2) == 2
    flip_cos = ((quadrant + 1) & 2) == 2
    sine = jnp.where(odd, cos_part, sin_part)
    cosine = jnp.where(odd, sin_part, cos_part)
    return jnp.where(flip_cos, -cosine, cosine), jnp.where(flip_sin, -sine, sine)


def body(
    img_ref,
    proj_ref,
    curve_ref,
    noise_ref,
    group_ref,
    shift_ref,
    orient_ref,
    prior_ref,
    cls_ref,
    con_ref,
    ev_ref,
    xbuf,
    pmain,
    prest,
    ctab,
    stab,
    crest,
    srest,
    smain,
    shrest,
    score,
    wts,
    stat,
    core_out,
    core_in,
    rest_out,
    rest_in,
    x_out,
    x_near_a,
    x_near_b,
    x_in,
    held,
    z_out,
    z_relay,
    z_in,
    z_core,
    ag_u_s,
    ag_d_s,
    ag_z_r,
    ag_y_s,
    ag_y_r,
    ag_f_s,
    ag_f_r,
    st_s,
    st_r,
    co_s,
    co_r,
    xs_s,
    xs_r,
    zs_s,
    zs_r,
):
    img = lax.axis_index("img")
    ref = lax.axis_index("ref")
    x = lax.div(img, 8)
    h = lax.rem(lax.div(img, 2), 4)
    d = lax.rem(img, 2)
    o = 1 - d
    y = lax.div(ref, 4)
    l = lax.rem(ref, 4)

    def ring(v):
        return lax.rem(v + 4, 4)

    def dev(img_at=img, ref_at=ref):
        return {"img": img_at, "ref": ref_at}

    def at_img(xx, hh, dd):
        return dev(img_at=(xx * 4 + hh) * 2 + dd)

    def copy(src, dst, send, recv, to):
        return pltpu.make_async_remote_copy(
            src_ref=src, dst_ref=dst, send_sem=send, recv_sem=recv, device_id=to, device_id_type=MESH
        )

    barrier = pltpu.get_barrier_semaphore()
    peers = [dev(ref_at=lax.rem(ref + k, 16)) for k in range(1, 16)]
    peers += [at_img(x, h, o), at_img(ring(x + 1), h, d), at_img(ring(x - 1), h, d)]
    for hh in (ring(h + 1), ring(h - 1)):
        peers += [at_img(x, hh, d), at_img(x, hh, o)]
    for peer in peers:
        pl.semaphore_signal(barrier, inc=1, device_id=peer, device_id_type=MESH)

    lane = lax.broadcasted_iota(jnp.int32, (1, 128), 1)

    def noise_row(tile, count):
        return jnp.concatenate([noise_ref[pl.ds(tile + t, 1), :] for t in range(count)], axis=1)


    group_row = group_ref[...].astype(F32)
    group_row = jnp.concatenate([group_row, group_row], axis=1)
    group_col = jnp.transpose(jnp.broadcast_to(group_row, (128, 128)))[:NIMG, :]
    start = pl.multiple_of(ref * 256, 128)
    turn = lax.rem(384 - 8 * ref, 384)
    curve_here = pltpu.roll(curve_ref[:, pl.ds(start, 384)], turn, 1)
    noise_here = pltpu.roll(jnp.broadcast_to(noise_row(2 * ref, 3), (8, 384)), turn, 1)[:1, :]
    parts = []
    for tile in range(3):
        span = slice(tile * 128, tile * 128 + 128)
        gain = jnp.zeros((NIMG, 128), F32)
        for g in range(GROUPS):
            gain = jnp.where(group_col == float(g), curve_here[g : g + 1, span], gain)
        gain = gain * noise_here[:, span]
        parts.append(img_ref[:, span].astype(F32) * jnp.concatenate([gain, gain], axis=0))
    second = pltpu.roll(jnp.concatenate(parts[1:], axis=1), 252, 1)[:, :128]
    rest = jnp.transpose(jnp.where(lane < 4, parts[1], parts[2]))[:16, :]
    row16 = lax.broadcasted_iota(jnp.int32, (16, 128), 0)
    rest = jnp.where(row16 < 8, rest, 0.0)
    xbuf[ref, 0:128, :] = parts[0].astype(BF16)
    xbuf[ref, 128:256, :] = second.astype(BF16)
    xbuf[ref, 256:272, :] = rest.astype(BF16)

    pl.semaphore_wait(barrier, len(peers))

    col_1 = jnp.where(l == 0, 1, l - 1)
    col_2 = jnp.where(l < 2, 2, jnp.where(l == 2, 3, 1))
    col_3 = jnp.where(l < 2, 3, 0)
    columns = [l, col_1, col_2, col_3]

    def shard(yy, e):
        return yy * 4 + columns[e]

    def z_copy_of(col, up):
        block = xbuf.at[y * 4 + col]
        to = dev(ref_at=y * 4 + lax.rem(l + (1 if up else 3), 4))
        return copy(block, block, (ag_u_s if up else ag_d_s).at[col], ag_z_r.at[col], to)

    def forward(col, start):
        @pl.when((col <= l) & (l < 3))
        def _():
            c = z_copy_of(col, True)
            c.start() if start else c.wait_send()

        @pl.when((col >= l) & (l > 0))
        def _():
            c = z_copy_of(col, False)
            c.start() if start else c.wait_send()

    y_up, y_down, y_far = ring(y + 1), ring(y - 1), ring(y + 2)

    def y_copy(way, e, src_y):
        to = dev(ref_at=(y_up if way == 0 else y_down) * 4 + l)
        block = xbuf.at[shard(src_y, e)]
        return copy(block, block, ag_y_s.at[way, e], ag_y_r.at[way, e], to)

    def f_copy(way, e, src_y):
        to = dev(ref_at=(y_up if way == 0 else y_down) * 4 + l)
        rows = pl.ds(0, 144) if way == 0 else pl.ds(144, 128)
        block = xbuf.at[shard(src_y, e), rows]
        return copy(block, block, ag_f_s.at[way, e], ag_f_r.at[way, e], to)

    y_copy(0, 0, y).start()
    y_copy(1, 0, y).start()
    forward(l, True)

    def take_z(e):
        z_copy_of(columns[e], True).wait_recv()
        forward(columns[e], True)
        y_copy(0, e, y).start()
        y_copy(1, e, y).start()

    def take_y(e):
        y_copy(0, e, y_down).wait_recv()
        f_copy(0, e, y_down).start()
        y_copy(1, e, y_up).wait_recv()
        f_copy(1, e, y_up).start()

    def take_far(e):
        f_copy(0, e, y_far).wait_recv()
        f_copy(1, e, y_far).wait_recv()

    def table(pixel, width):
        srow = lax.broadcasted_iota(jnp.int32, (8, width), 0) + 1
        move_x = jnp.zeros((8, width), jnp.int32)
        move_y = jnp.zeros((8, width), jnp.int32)
        for s in range(1, NSHIFT):
            move_x = jnp.where(srow == s, shift_ref[0, s], move_x)
            move_y = jnp.where(srow == s, shift_ref[1, s], move_y)
        freq_x = pixel & (BOX // 2 - 1)
        freq_y = lax.shift_right_logical(pixel, 6) - NPIX // BOX
        return sincos((move_x * freq_x + move_y * freq_y) & (BOX - 1))

    def table_step(b, carry):
        at = lax.broadcasted_iota(jnp.int32, (8, 256), 1)
        pixel = 264 * b + at + jnp.where(at >= 128, 4, 0)
        cosine, sine = table(pixel, 256)
        ctab[b] = cosine
        stab[b] = sine
        return carry

    lax.fori_loop(0, 16, table_step, 0)
    at = lax.broadcasted_iota(jnp.int32, (8, 128), 1)
    cosine, sine = table(132 * lax.shift_right_logical(at, 2) + 128 + (at & 3), 128)
    crest[...] = cosine
    srest[...] = sine

    def proj_step(b, carry):
        out = []
        for c in range(2):
            kept = carry[c]
            for u in range(2):
                n = 2 * b + u
                window = proj_ref[c, :, pl.ds(pl.multiple_of(n * 128, 128), 256)].astype(F32)
                turned = pltpu.roll(window, lax.rem(256 - 4 * n, 256), 1)
                pmain[b, c, :, u * 128 : u * 128 + 128] = turned[:, :128].astype(BF16)
                kept = jnp.where(lax.shift_right_logical(lane, 2) == n, window[:, 128:], kept)
            out.append(kept)
        return tuple(out)

    zero_rest = jnp.zeros((NPROJ, 128), F32)
    rests = lax.fori_loop(0, 16, proj_step, (zero_rest, zero_rest))
    for c in range(2):
        prest[c] = rests[c].astype(BF16)

    take_z(1)
    take_y(0)

    def norm_step(t, total):
        span = pl.ds(pl.multiple_of(t * 384, 128), 384)
        re = proj_ref[0, :, span].astype(F32)
        im = proj_ref[1, :, span].astype(F32)
        curve = curve_ref[:, span]
        gain = 0.5 * (curve * curve * noise_row(3 * t, 3))
        power = re * re + im * im
        return total + lax.dot_general(
            two_parts(power), two_parts(gain), NT, preferred_element_type=F32
        )

    def two_parts(value):
        high = value.astype(BF16)
        return jnp.concatenate([high, (value - high.astype(F32)).astype(BF16)], axis=0)

    norm = lax.fori_loop(0, 11, norm_step, jnp.zeros((2 * NPROJ, 2 * GROUPS), F32))
    norm = norm[:NPROJ] + norm[NPROJ:]
    norm = norm[:, :GROUPS] + norm[:, GROUPS:]
    grow = lax.broadcasted_iota(jnp.int32, (GROUPS, 128), 0)
    members = (group_row == grow.astype(F32)).astype(F32)
    penalty = jnp.dot(norm, members, precision=HIGHEST, preferred_element_type=F32)
    orient_row = jnp.concatenate([orient_ref[...].astype(F32), jnp.zeros((1, 80), F32)], axis=1)
    orient_col = jnp.transpose(jnp.broadcast_to(orient_row, (128, 128)))[:NPROJ, :]
    prior = jnp.zeros((NPROJ, 1), F32)
    for half in range(2):
        hit = orient_col == (lane + half * 128).astype(F32)
        prior += jnp.sum(
            jnp.where(hit, prior_ref[half : half + 1, :], 0.0), axis=1, keepdims=True
        )
    base = prior - penalty

    score[...] = jnp.zeros_like(score)
    take_z(2)
    take_y(1)

    def process(b):
        for t in range(2):
            span = slice(t * 128, t * 128 + 128)
            re = xbuf[b, t * 128 : t * 128 + 64, :]
            im = xbuf[b, t * 128 + 64 : t * 128 + 128, :]
            smain[b, 0, 0:NIMG, span] = re
            smain[b, 1, 0:NIMG, span] = im
            re = re.astype(F32)
            im = im.astype(F32)
            for s in range(1, NSHIFT):
                rows = slice(s * NIMG, s * NIMG + NIMG)
                cosine = ctab[b, s - 1 : s, span]
                sine = stab[b, s - 1 : s, span]
                smain[b, 0, rows, span] = (re * cosine + im * sine).astype(BF16)
                smain[b, 1, rows, span] = (im * cosine - re * sine).astype(BF16)
        score[...] += lax.dot_general(
            smain[b, 0], pmain[b, 0], NT, preferred_element_type=F32
        ) + lax.dot_general(smain[b, 1], pmain[b, 1], NT, preferred_element_type=F32)

    def process_all(blocks):
        def step(t, carry):
            b = blocks[0]
            for k in range(1, len(blocks)):
                b = jnp.where(t == k, blocks[k], b)
            process(b)
            return carry

        lax.fori_loop(0, len(blocks), step, 0)

    process_all([shard(y, 0), shard(y, 1), shard(y_down, 0), shard(y_up, 0)])
    take_z(3)
    take_y(2)
    take_far(0)
    process_all([shard(y, 2), shard(y_down, 1), shard(y_up, 1), shard(y_far, 0)])
    take_y(3)
    take_far(1)
    process_all([shard(y, 3), shard(y_down, 2), shard(y_up, 2), shard(y_far, 1)])
    process_all([shard(y_down, 3), shard(y_up, 3)])
    take_far(2)
    process(shard(y_far, 2))
    take_far(3)
    process(shard(y_far, 3))

    rest_t = jnp.concatenate([xbuf[b, 256:272, :].astype(F32)[:8] for b in range(16)], axis=0)
    rest_x = jnp.transpose(rest_t)
    re, im = rest_x[:NIMG], rest_x[NIMG:]
    shrest[0, 0:NIMG, :] = re.astype(BF16)
    shrest[1, 0:NIMG, :] = im.astype(BF16)
    for s in range(1, NSHIFT):
        rows = slice(s * NIMG, s * NIMG + NIMG)
        cosine = crest[s - 1 : s, :]
        sine = srest[s - 1 : s, :]
        shrest[0, rows, :] = (re * cosine + im * sine).astype(BF16)
        shrest[1, rows, :] = (im * cosine - re * sine).astype(BF16)
    full = (
        score[...]
        + lax.dot_general(shrest[0], prest[0], NT, preferred_element_type=F32)
        + lax.dot_general(shrest[1], prest[1], NT, preferred_element_type=F32)
    )
    full = jnp.concatenate([full, jnp.zeros((ROWS, 128 - NPROJ), F32)], axis=1)

    tiles = []
    for t in range(5):
        if t < 4:
            tiles.append(jnp.transpose(full[t * 128 : t * 128 + 128])[:NPROJ] + base)
        else:
            last = jnp.concatenate([full[512:576], jnp.zeros((64, 128), F32)], axis=0)
            tiles.append(jnp.where(lane < 64, jnp.transpose(last)[:NPROJ] + base, -3e38))
    high = tiles[0]
    for t in range(1, 5):
        high = jnp.maximum(high, tiles[t])
    high = jnp.max(high, axis=0, keepdims=True)
    high = jnp.maximum(high, pltpu.roll(jnp.broadcast_to(high, (8, 128)), 64, 1)[:1])
    total = jnp.exp(tiles[0] - high)
    for t in range(1, 5):
        total += jnp.exp(tiles[t] - high)
    total = jnp.sum(total, axis=0, keepdims=True)
    total = total + pltpu.roll(jnp.broadcast_to(total, (8, 128)), 64, 1)[:1]
    row8 = lax.broadcasted_iota(jnp.int32, (8, 128), 0)
    stat[ref] = jnp.where(row8 == 0, high, total)
    st_copies = []
    for k in range(1, 16):
        st_copies.append(
            copy(stat.at[ref], stat.at[ref], st_s.at[k], st_r.at[k], dev(ref_at=lax.rem(ref + k, 16)))
        )
    for c in st_copies:
        c.start()
    for k in range(1, 16):
        src = lax.rem(ref + 16 - k, 16)
        copy(stat.at[src], stat.at[src], st_s.at[k], st_r.at[k], dev(ref_at=src)).wait_recv()
    highest = stat[0, 0:1, :]
    for b in range(1, 16):
        highest = jnp.maximum(highest, stat[b, 0:1, :])
    whole = jnp.zeros((1, 128), F32)
    for b in range(16):
        whole += stat[b, 1:2, :] * jnp.exp(stat[b, 0:1, :] - highest)
    evidence = highest + jnp.log(whole)
    ev_ref[...] = evidence
    for t in range(5):
        w = jnp.exp(tiles[t] - evidence).astype(BF16)
        if t < 4:
            wts[:, t * 128 : t * 128 + 128] = w
        else:
            wts[:, 512:576] = w[:, :64]
    members_all = jnp.concatenate([members.astype(BF16)] * 4 + [members[:, :64].astype(BF16)], axis=1)
    group_sum = lax.dot_general(members_all, wts[...], NT, preferred_element_type=F32)
    group_sum = jnp.concatenate([group_sum, jnp.zeros((GROUPS, 80), F32)], axis=1)

    other = at_img(x, h, o)
    rest_out[0:48, :] = jnp.dot(wts[...], shrest[o], preferred_element_type=F32).astype(BF16)
    rest_out[48:64, :] = group_sum.astype(BF16)
    rest_copy = copy(rest_out, rest_in, co_s.at[4], co_r.at[4], other)
    rest_copy.start()

    order = [ring(x + 2), ring(x + 1), ring(x + 3), x]
    runs = [ring(h + 2), ring(h + 1), ring(h + 3), h]

    def core_copy(i):
        return copy(core_out.at[i], core_in.at[i], co_s.at[i], co_r.at[i], other)

    def other_chunk(i):
        for u in range(4):
            got = jnp.dot(wts[...], smain[4 * order[i] + runs[u], o], preferred_element_type=F32)
            for v in range(2):
                r = PIECE * (2 * u + v)
                core_out[i, r : r + PIECE, :] = got[:, v * 128 : v * 128 + 128].astype(BF16)
        core_copy(i).start()

    other_chunk(0)
    other_chunk(1)

    rest_sum = jnp.dot(wts[...], shrest[d], preferred_element_type=F32)
    rest_copy.wait_recv()
    rest_sum = rest_sum + rest_in[0:48, :].astype(F32)
    group_sum = group_sum + rest_in[48:64, :].astype(F32)

    def left(value, by):
        return pltpu.roll(value, lax.rem(256 - by, 128), 1)

    group_half = left(group_sum, 32 + 24 * d)

    def packed(q):
        out = left(rest_sum[0:16], 32 * q)
        out = jnp.where(lane < 32, out, left(rest_sum[16:32], 32 * q - 32))
        out = jnp.where(lane < 64, out, left(rest_sum[32:48], 32 * q - 64))
        return jnp.where(lane < 96, out, group_half)

    def piece_row(k):
        return 16 + PIECE * k

    def own_chunk(i, store):
        q = order[i]
        core_copy(i).wait_recv()
        for u in range(4):
            got = jnp.dot(wts[...], smain[4 * q + runs[u], d], preferred_element_type=F32)
            for v in range(2):
                k = 2 * u + v
                r = PIECE * k
                store(k, got[:, v * 128 : v * 128 + 128] + core_in[i, r : r + PIECE, :].astype(F32))
        store(-1, packed(q))

    x_up, x_down = at_img(ring(x + 1), h, d), at_img(ring(x - 1), h, d)

    def rows_of(k):
        return slice(0, 16) if k < 0 else slice(piece_row(k), piece_row(k) + PIECE)

    def store_far(k, value):
        x_out[0, rows_of(k), :] = value.astype(BF16)

    own_chunk(0, store_far)
    near_a = copy(x_out.at[0, pl.ds(0, HALF)], x_near_a, xs_s.at[0], xs_r.at[0], x_up)
    near_b = copy(x_out.at[0, pl.ds(HALF, MSG - HALF)], x_near_b, xs_s.at[1], xs_r.at[1], x_down)
    near_a.start()
    near_b.start()

    def store_up(k, value):
        held[rows_of(k), :] = value

    def x_copy(way, part):
        rows = pl.ds(0, FIRST) if part == 0 else pl.ds(FIRST, MSG - FIRST)
        k = 2 + 2 * way + part
        to = x_up if way == 0 else x_down
        return copy(x_out.at[1 + way, rows], x_in.at[way, rows], xs_s.at[k], xs_r.at[k], to)

    other_chunk(2)
    own_chunk(1, store_up)
    x_out[1, HALF:MSG, :] = held[HALF:MSG, :].astype(BF16)
    near_a.wait_recv()
    x_out[1, 0:HALF, :] = (held[0:HALF, :] + x_near_a[...].astype(F32)).astype(BF16)
    x_copy(0, 0).start()
    x_copy(0, 1).start()

    other_chunk(3)
    own_chunk(2, store_up)
    x_out[2, 0:HALF, :] = held[0:HALF, :].astype(BF16)
    x_copy(1, 0).start()
    near_b.wait_recv()
    x_out[2, HALF:MSG, :] = (held[HALF:MSG, :] + x_near_b[...].astype(F32)).astype(BF16)
    x_copy(1, 1).start()

    own_chunk(3, store_up)

    def add_x(part):
        rows = slice(0, FIRST) if part == 0 else slice(FIRST, MSG)
        x_copy(0, part).wait_recv()
        x_copy(1, part).wait_recv()
        held[rows, :] += x_in[0, rows, :].astype(F32) + x_in[1, rows, :].astype(F32)

    add_x(0)

    def piece_of(u, dd):
        return held[pl.ds(pl.multiple_of(16 + PIECE * (2 * u + dd), 16), PIECE), :]

    rest_pack = held[0:16, :]
    h_up, h_down = ring(h + 1), ring(h - 1)

    def fill(slot, value, extra):
        z_out[slot, 0:48, :] = value.astype(BF16)
        z_out[slot, 48:64, :] = extra.astype(BF16)

    fill(0, piece_of(0, 0), rest_pack)
    fill(1, piece_of(0, 1), rest_pack)
    relay_up = copy(z_out.at[0], z_relay.at[0], zs_s.at[0], zs_r.at[0], at_img(x, h_up, d))
    relay_down = copy(z_out.at[1], z_relay.at[1], zs_s.at[1], zs_r.at[1], at_img(x, h_down, d))
    relay_up.start()
    relay_down.start()
    add_x(1)

    def z_copy(slot):
        way, dd = (slot - 2) // 2, (slot - 2) % 2
        to = at_img(x, h_up if way == 0 else h_down, dd)
        return copy(z_out.at[slot], z_in.at[way, d], zs_s.at[slot], zs_r.at[2 + 2 * way + d], to)

    fill(3, piece_of(1, 1), rest_pack)
    z_copy(3).start()
    fill(4, piece_of(2, 0), rest_pack)
    z_copy(4).start()
    fill(6, piece_of(3, o), rest_pack)
    core_last = copy(z_out.at[6], z_core, zs_s.at[6], zs_r.at[6], other)
    core_last.start()
    relay_up.wait_recv()
    fill(
        2,
        piece_of(1, 0) + z_relay[0, 0:48, :].astype(F32),
        rest_pack + z_relay[0, 48:64, :].astype(F32),
    )
    z_copy(2).start()
    relay_down.wait_recv()
    fill(
        5,
        piece_of(2, 1) + z_relay[1, 0:48, :].astype(F32),
        rest_pack + z_relay[1, 48:64, :].astype(F32),
    )
    z_copy(5).start()

    mine = jnp.concatenate([piece_of(3, d), rest_pack], axis=0)
    core_last.wait_recv()
    theirs = z_core[...].astype(F32)
    for way in range(2):
        for c in range(2):
            slot = z_in.at[way, c]
            copy(slot, slot, zs_s.at[2], zs_r.at[2 + 2 * way + c], other).wait_recv()
    local = 2 * h + d
    packs = []
    for c in range(2):
        both = jnp.where(d == c, mine, theirs)
        both = both + z_in[0, c].astype(F32) + z_in[1, c].astype(F32)
        cls_ref[c, :, 0:128] = both[0:48]
        pack = both[48:64]
        packs.append(pack)
        for a in range(3):
            cls_ref[c, 16 * a : 16 * a + 16, 128:256] = left(pack, 32 * a + 4 * local)
    group_all = jnp.where(lane < 24, left(packs[0], 96), left(packs[1], 72))
    group_all = jnp.where(lane < 48, group_all, 0.0)
    span = pl.ds(pl.multiple_of(img * 128, 128), 256)
    turn = lax.rem(256 - 4 * img, 256)
    curve = curve_ref[:, span]
    gain = pltpu.roll(curve * curve * noise_row(img, 2), turn, 1)
    contrast = lax.dot_general(
        jnp.transpose(jnp.concatenate([group_all, jnp.zeros((112, 128), F32)], axis=0))[:NPROJ, :GROUPS],
        gain,
        (((1,), (0,)), ((), ())),
        precision=HIGHEST,
        preferred_element_type=F32,
    )
    con_ref[...] = contrast

    for e in range(4):
        forward(columns[e], False)
        for way in range(2):
            y_copy(way, e, y).wait_send()
            f_copy(way, e, y).wait_send()
    for c in st_copies:
        c.wait_send()
    for i in range(4):
        core_copy(i).wait_send()
    for c in (rest_copy, near_a, near_b, relay_up, relay_down, core_last):
        c.wait_send()
    for way in range(2):
        for part in range(2):
            x_copy(way, part).wait_send()
    for slot in range(2, 6):
        z_copy(slot).wait_send()


def on_device(
    images, projections, contrast_curve, noise_weight, defocus_group, shifts, orient_index, orient_prior
):
    rows = jnp.pad(images.transpose(1, 0, 2).reshape(2 * NIMG, 264), ((0, 0), (0, 120)))
    vmem = pl.BlockSpec(memory_space=pltpu.VMEM)
    sem = pltpu.SemaphoreType.DMA
    cls, con, ev = pl.pallas_call(
        body,
        out_shape=(
            jax.ShapeDtypeStruct((2, NPROJ, 256), F32),
            jax.ShapeDtypeStruct((NPROJ, 256), F32),
            jax.ShapeDtypeStruct((1, 128), F32),
        ),
        in_specs=[vmem, vmem, vmem, vmem, vmem, pl.BlockSpec(memory_space=pltpu.SMEM), vmem, vmem],
        out_specs=(vmem, vmem, vmem),
        scratch_shapes=[
            pltpu.VMEM((16, SHARD, 128), BF16),
            pltpu.VMEM((16, 2, NPROJ, 256), BF16),
            pltpu.VMEM((2, NPROJ, 128), BF16),
            pltpu.VMEM((16, 8, 256), F32),
            pltpu.VMEM((16, 8, 256), F32),
            pltpu.VMEM((8, 128), F32),
            pltpu.VMEM((8, 128), F32),
            pltpu.VMEM((16, 2, ROWS, 256), BF16),
            pltpu.VMEM((2, ROWS, 128), BF16),
            pltpu.VMEM((ROWS, NPROJ), F32),
            pltpu.VMEM((NPROJ, ROWS), BF16),
            pltpu.VMEM((16, 8, 128), F32),
            pltpu.VMEM((4, 8 * PIECE, 128), BF16),
            pltpu.VMEM((4, 8 * PIECE, 128), BF16),
            pltpu.VMEM((64, 128), BF16),
            pltpu.VMEM((64, 128), BF16),
            pltpu.VMEM((3, MSG, 128), BF16),
            pltpu.VMEM((HALF, 128), BF16),
            pltpu.VMEM((MSG - HALF, 128), BF16),
            pltpu.VMEM((2, MSG, 128), BF16),
            pltpu.VMEM((MSG, 128), F32),
            pltpu.VMEM((7, 64, 128), BF16),
            pltpu.VMEM((2, 64, 128), BF16),
            pltpu.VMEM((2, 2, 64, 128), BF16),
            pltpu.VMEM((64, 128), BF16),
            sem((4,)),
            sem((4,)),
            sem((4,)),
            sem((2, 4)),
            sem((2, 4)),
            sem((2, 4)),
            sem((2, 4)),
            sem((16,)),
            sem((16,)),
            sem((5,)),
            sem((5,)),
            sem((6,)),
            sem((6,)),
            sem((7,)),
            sem((7,)),
        ],
        compiler_params=pltpu.CompilerParams(
            collective_id=0, has_side_effects=True, vmem_limit_bytes=40 * 1024 * 1024
        ),
        name="expectation",
    )(
        rows,
        projections.transpose(1, 0, 2),
        contrast_curve,
        noise_weight.reshape(NPIX // 128, 128),
        defocus_group.reshape(1, NIMG),
        shifts.T,
        orient_index.reshape(1, NPROJ),
        orient_prior.reshape(2, 128),
    )
    return cls[:, :, :132].transpose(1, 0, 2), con[:, :132], ev[0, :NIMG]


def solution(mesh):
    in_specs = (P("img", None, "ref"), P("ref", None, None), P(), P(), P("img"), P(), P("ref"), P())
    out_specs = (P("ref", None, "img"), P("ref", "img"), P("img"))
    return jax.shard_map(
        on_device, mesh=mesh, in_specs=in_specs, out_specs=out_specs, check_vma=False
    )
```

time: 592 us -> 66.5 us (0.11)
  waiting for transfers between devices: 337 us -> 0 us
  blocking collectives: 177 us -> 0 us
  Pallas kernels: 0 us -> 60.8 us
  other arithmetic: 23.9 us -> 0 us
  local copies, waits for them, and re-layouts: 21.8 us -> 4.69 us
  matrix products: 15.7 us -> 0 us
  between operations: 15.1 us -> 0.74 us
    unnamed x3 -> x0, waiting for transfers between devices: 253 us -> none
    psum x2 -> x0, blocking collectives: 142 us -> none  [the longest x1 110 us: on_device(): per_group = lax.psum(per_group, 'img')]
    all_gather x1 -> x0, waiting for transfers between devices: 84.6 us -> none  [on_device(): gathered = lax.all_gather(images, 'ref', axis=2, tiled=True)]
    pallas_call x0 -> x1, Pallas kernels: none -> 60.8 us  [on_device(): pl.pallas_call(body, out_shape=(jax.ShapeDtypeStruct((2, NPROJ, 256), F32...]
    pmax x1 -> x0, blocking collectives: 35.6 us -> none  [on_device(): highest = lax.pmax(local_high, 'ref')]
    dot_general x24 -> x0, matrix products: 15.7 us -> none  [the longest x9 9.5 us: on_device(): jnp.einsum('ik,jk->ij', shift_layer, flat_proj, preferred_element_type=jn...]
    reduce_max x10 -> x0, other arithmetic: 10 us -> none  [on_device(): local_high = jnp.max(scores, axis=(0, 2))]
    unnamed x61 -> x15, local copies, waits for them, and re-layouts: 12.8 us -> 3.25 us
  transfers between devices with their start and end apart: 2 -> 0, of which waited for: 2 -> 0; matrix products, arithmetic and copies ran while one was open for 1% -> 0% of each run, Pallas kernels for 0% -> 0%
where the time goes in v1:
time: 66.5 us; the launch traced here: 66.3 us
  Pallas kernels  60.8 us (91%)
  local copies, waits for them, and re-layouts  4.69 us (7%)
  between operations  0.74 us (1%)
    pallas_call x1, Pallas kernels, on_device(): pl.pallas_call(body, out_shape=(jax.ShapeDtypeStruct((2, NPROJ, 256), F32...  60.8 us
    unnamed x15, local copies, waits for them, and re-layouts  3.25 us

profile of v1, /device:TPU:1, one launch (start us, length us, event | category | flops | bytes accessed | tf_op | source)
XLA Modules:
  0.0 66.3 jit_solution(16167209959230590227)
XLA Ops:
  0.6 0.9 %copy.11 = bf16[2,64,264]{2,1,0:T(8,128)(2,1)S(1)} copy(bf16[2,64,264]{2,0,1:T(2,128)(2,1)} %bitcast.23) | data formatting | bytes 135168 | tf_op jit(solution)/shard_map/transpose | solution.py:610
  1.6 0.0 copy-start
  1.6 0.0 copy-start.1
  1.6 0.0 copy-start.3
  1.6 0.0 copy-start.5
  1.6 1.3 %copy.15 = bf16[48,2,4224]{2,0,1:T(8,128)(2,1)S(1)} copy(bf16[48,2,4224]{2,1,0:T(2,128)(2,1)} %param.9) | data formatting | bytes 1622016 | tf_op args[1]
  2.9 0.0 copy-start.2
  2.9 0.0 copy-start.4
  2.9 0.0 copy-done
  2.9 0.0 copy-done.1
  2.9 0.0 copy-done.3
  2.9 0.0 copy-done.5
  2.9 0.6 copy-done.2
  3.6 0.0 copy-done.4
  3.6 60.8 %expectation.1 = (f32[2,48,256]{2,1,0:T(8,128)S(1)}, f32[48,256]{1,0:T(8,128)S(1)}, f32[1,128]{1,0:T(1,128)S(1)}) custom-call(bf16[128,384]{1,0:T(8,128)(2,1)S(1)} %pad.4.img_ref, bf16[2,48,4224]{2,1,0:T(8,128)(2,1)S(1)} %bitcast.15, f32[16,4224]{1,0:T(8,128)S(1)} %copy-done, f32[33,128]{1,0:T(8,128)S(1)} %bitcast.17, s32[1,64]{1,0:T(1,128)S(1)} %bitcast.20, ...), custom_call_target="tpu_custom_call" | custom-call | tf_op jit(solution)/shard_map/expectation/pallas_call | solution.py:613
  64.4 0.7 %copy.13 = f32[48,2,132]{2,1,0:T(2,128)} copy(f32[48,2,132]{2,0,1:T(8,128)S(1)} %slice_bitcast_fusion) | data formatting | bytes 101376
  65.1 0.5 slice_bitcast_fusion.1
  65.7 0.6 copy.17
  (2 shorter events, 0.0 us)
Async XLA Ops:
  1.6 1.3 %copy-start = (f32[16,4224]{1,0:T(8,128)S(1)}, f32[16,4224]{1,0:T(8,128)}, u32[]{:S(2)}) copy-start(f32[16,4224]{1,0:T(8,128)} %curve_ref.1) | copy-start | bytes 811012
  1.6 1.3 %copy-start.1 = (f32[4224]{0:T(1024)S(1)}, f32[4224]{0:T(1024)}, u32[]{:S(2)}) copy-start(f32[4224]{0:T(1024)} %param.11) | copy-start | bytes 50692
  1.6 1.3 %copy-start.3 = (f32[256]{0:T(256)S(1)}, f32[256]{0:T(256)}, u32[]{:S(2)}) copy-start(f32[256]{0:T(256)} %param.15) | copy-start | bytes 3076
  1.6 1.3 %copy-start.5 = (s32[48]{0:T(128)S(1)}, s32[48]{0:T(128)}, u32[]{:S(2)}) copy-start(s32[48]{0:T(128)} %param.14) | copy-start | bytes 580
  2.9 0.7 %copy-start.2 = (s32[9,2]{0,1:T(2,128)S(1)}, s32[9,2]{0,1:T(2,128)}, u32[]{:S(2)}) copy-start(s32[9,2]{0,1:T(2,128)} %param.13) | copy-start | bytes 220
  2.9 0.7 %copy-start.4 = (s32[64]{0:T(128)S(1)}, s32[64]{0:T(128)}, u32[]{:S(2)}) copy-start(s32[64]{0:T(128)} %param.12) | copy-start | bytes 772

commit v2 on v1

--- a/solution.py
+++ b/solution.py
@@ -46,59 +46,9 @@
     return jnp.where(flip_cos, -cosine, cosine), jnp.where(flip_sin, -sine, sine)
 
 
-def body(
-    img_ref,
-    proj_ref,
-    curve_ref,
-    noise_ref,
-    group_ref,
-    shift_ref,
-    orient_ref,
-    prior_ref,
-    cls_ref,
-    con_ref,
-    ev_ref,
-    xbuf,
-    pmain,
-    prest,
-    ctab,
-    stab,
-    crest,
-    srest,
-    smain,
-    shrest,
-    score,
-    wts,
-    stat,
-    core_out,
-    core_in,
-    rest_out,
-    rest_in,
-    x_out,
-    x_near_a,
-    x_near_b,
-    x_in,
-    held,
-    z_out,
-    z_relay,
-    z_in,
-    z_core,
-    ag_u_s,
-    ag_d_s,
-    ag_z_r,
-    ag_y_s,
-    ag_y_r,
-    ag_f_s,
-    ag_f_r,
-    st_s,
-    st_r,
-    co_s,
-    co_r,
-    xs_s,
-    xs_r,
-    zs_s,
-    zs_r,
-):
+def gather(img_ref, proj_ref, curve_ref, noise_ref, group_ref, shift_ref, orient_ref, prior_ref,
+    smain, shrest, wts, gsum_ref, ev_ref,
+    xbuf, pmain, prest, ctab, stab, crest, srest, score, stat, ag_z_s, ag_z_r, ag_y_s, ag_y_r, ag_f_s, ag_f_r, st_s, st_r):
     img = lax.axis_index("img")
     ref = lax.axis_index("ref")
     x = lax.div(img, 8)
@@ -124,12 +74,8 @@
 
     barrier = pltpu.get_barrier_semaphore()
     peers = [dev(ref_at=lax.rem(ref + k, 16)) for k in range(1, 16)]
-    peers += [at_img(x, h, o), at_img(ring(x + 1), h, d), at_img(ring(x - 1), h, d)]
-    for hh in (ring(h + 1), ring(h - 1)):
-        peers += [at_img(x, hh, d), at_img(x, hh, o)]
     for peer in peers:
         pl.semaphore_signal(barrier, inc=1, device_id=peer, device_id_type=MESH)
-
     lane = lax.broadcasted_iota(jnp.int32, (1, 128), 1)
 
     def noise_row(tile, count):
@@ -161,58 +107,56 @@
 
     pl.semaphore_wait(barrier, len(peers))
 
-    col_1 = jnp.where(l == 0, 1, l - 1)
-    col_2 = jnp.where(l < 2, 2, jnp.where(l == 2, 3, 1))
-    col_3 = jnp.where(l < 2, 3, 0)
-    columns = [l, col_1, col_2, col_3]
+    columns = [lax.rem(l + 4 - e, 4) for e in range(4)]
+    halves = (pl.ds(0, 144), pl.ds(144, 128))
 
     def shard(yy, e):
         return yy * 4 + columns[e]
 
-    def z_copy_of(col, up):
-        block = xbuf.at[y * 4 + col]
-        to = dev(ref_at=y * 4 + lax.rem(l + (1 if up else 3), 4))
-        return copy(block, block, (ag_u_s if up else ag_d_s).at[col], ag_z_r.at[col], to)
-
-    def forward(col, start):
-        @pl.when((col <= l) & (l < 3))
-        def _():
-            c = z_copy_of(col, True)
-            c.start() if start else c.wait_send()
-
-        @pl.when((col >= l) & (l > 0))
-        def _():
-            c = z_copy_of(col, False)
-            c.start() if start else c.wait_send()
+    def z_send(e, part):
+        block = xbuf.at[ref, halves[part]]
+        to = dev(ref_at=y * 4 + lax.rem(l + e, 4))
+        return copy(block, block, ag_z_s.at[e, part], ag_z_r.at[e, part], to)
 
     y_up, y_down, y_far = ring(y + 1), ring(y - 1), ring(y + 2)
 
-    def y_copy(way, e, src_y):
+    def y_copy(way, e, src_y, part):
         to = dev(ref_at=(y_up if way == 0 else y_down) * 4 + l)
-        block = xbuf.at[shard(src_y, e)]
-        return copy(block, block, ag_y_s.at[way, e], ag_y_r.at[way, e], to)
+        block = xbuf.at[shard(src_y, e), halves[part]]
+        return copy(block, block, ag_y_s.at[way, e, part], ag_y_r.at[way, e, part], to)
 
     def f_copy(way, e, src_y):
         to = dev(ref_at=(y_up if way == 0 else y_down) * 4 + l)
-        rows = pl.ds(0, 144) if way == 0 else pl.ds(144, 128)
-        block = xbuf.at[shard(src_y, e), rows]
+        block = xbuf.at[shard(src_y, e), halves[way]]
         return copy(block, block, ag_f_s.at[way, e], ag_f_r.at[way, e], to)
 
-    y_copy(0, 0, y).start()
-    y_copy(1, 0, y).start()
-    forward(l, True)
+    def send_y(e):
+        y_copy(0, e, y, 0).start()
+        y_copy(1, e, y, 1).start()
+        y_copy(0, e, y, 1).start()
+        y_copy(1, e, y, 0).start()
+
+    z_send(1, 0).start()
+    z_send(3, 0).start()
+    send_y(0)
+    z_send(1, 1).start()
+    z_send(3, 1).start()
+    z_send(2, 0).start()
+    z_send(2, 1).start()
 
     def take_z(e):
-        z_copy_of(columns[e], True).wait_recv()
-        forward(columns[e], True)
-        y_copy(0, e, y).start()
-        y_copy(1, e, y).start()
+        for part in range(2):
+            block = xbuf.at[shard(y, e), halves[part]]
+            copy(block, block, ag_z_s.at[e, part], ag_z_r.at[e, part], dev(ref_at=shard(y, e))).wait_recv()
+        send_y(e)
 
     def take_y(e):
-        y_copy(0, e, y_down).wait_recv()
+        y_copy(0, e, y_down, 0).wait_recv()
         f_copy(0, e, y_down).start()
-        y_copy(1, e, y_up).wait_recv()
+        y_copy(1, e, y_up, 1).wait_recv()
         f_copy(1, e, y_up).start()
+        y_copy(0, e, y_down, 1).wait_recv()
+        y_copy(1, e, y_up, 0).wait_recv()
 
     def take_far(e):
         f_copy(0, e, y_far).wait_recv()
@@ -261,8 +205,9 @@
     for c in range(2):
         prest[c] = rests[c].astype(BF16)
 
+    take_y(0)
     take_z(1)
-    take_y(0)
+    take_z(3)
 
     def norm_step(t, total):
         span = pl.ds(pl.multiple_of(t * 384, 128), 384)
@@ -296,8 +241,8 @@
     base = prior - penalty
 
     score[...] = jnp.zeros_like(score)
+    take_y(1)
     take_z(2)
-    take_y(1)
 
     def process(b):
         for t in range(2):
@@ -329,18 +274,17 @@
         lax.fori_loop(0, len(blocks), step, 0)
 
     process_all([shard(y, 0), shard(y, 1), shard(y_down, 0), shard(y_up, 0)])
-    take_z(3)
+    take_y(3)
+    take_far(0)
+    process_all([shard(y, 3), shard(y_down, 1), shard(y_up, 1), shard(y_far, 0)])
     take_y(2)
-    take_far(0)
-    process_all([shard(y, 2), shard(y_down, 1), shard(y_up, 1), shard(y_far, 0)])
-    take_y(3)
     take_far(1)
-    process_all([shard(y, 3), shard(y_down, 2), shard(y_up, 2), shard(y_far, 1)])
-    process_all([shard(y_down, 3), shard(y_up, 3)])
+    process_all([shard(y, 2), shard(y_down, 3), shard(y_up, 3), shard(y_far, 1)])
+    process_all([shard(y_down, 2), shard(y_up, 2)])
+    take_far(3)
+    process(shard(y_far, 3))
     take_far(2)
     process(shard(y_far, 2))
-    take_far(3)
-    process(shard(y_far, 3))
 
     rest_t = jnp.concatenate([xbuf[b, 256:272, :].astype(F32)[:8] for b in range(16)], axis=0)
     rest_x = jnp.transpose(rest_t)
@@ -404,9 +348,61 @@
         else:
             wts[:, 512:576] = w[:, :64]
     members_all = jnp.concatenate([members.astype(BF16)] * 4 + [members[:, :64].astype(BF16)], axis=1)
-    group_sum = lax.dot_general(members_all, wts[...], NT, preferred_element_type=F32)
-    group_sum = jnp.concatenate([group_sum, jnp.zeros((GROUPS, 80), F32)], axis=1)
-
+    gsum_ref[...] = lax.dot_general(members_all, wts[...], NT, preferred_element_type=F32)
+
+    for e in range(4):
+        for part in range(2):
+            if e:
+                z_send(e, part).wait_send()
+            for way in range(2):
+                y_copy(way, e, y, part).wait_send()
+        for way in range(2):
+            f_copy(way, e, y).wait_send()
+    for c in st_copies:
+        c.wait_send()
+
+
+def reduce(smain, shrest, wts, gsum_ref, curve_ref, noise_ref,
+    cls_ref, con_ref,
+    core_out, core_in, rest_out, rest_in, x_out, x_near_a, x_near_b, x_in, held, z_out, z_relay, z_in, z_core,
+    co_s, co_r, xs_s, xs_r, zs_s, zs_r):
+    img = lax.axis_index("img")
+    ref = lax.axis_index("ref")
+    x = lax.div(img, 8)
+    h = lax.rem(lax.div(img, 2), 4)
+    d = lax.rem(img, 2)
+    o = 1 - d
+    y = lax.div(ref, 4)
+    l = lax.rem(ref, 4)
+
+    def ring(v):
+        return lax.rem(v + 4, 4)
+
+    def dev(img_at=img, ref_at=ref):
+        return {"img": img_at, "ref": ref_at}
+
+    def at_img(xx, hh, dd):
+        return dev(img_at=(xx * 4 + hh) * 2 + dd)
+
+    def copy(src, dst, send, recv, to):
+        return pltpu.make_async_remote_copy(
+            src_ref=src, dst_ref=dst, send_sem=send, recv_sem=recv, device_id=to, device_id_type=MESH
+        )
+
+    barrier = pltpu.get_barrier_semaphore()
+    peers = [at_img(x, h, o), at_img(ring(x + 1), h, d), at_img(ring(x - 1), h, d)]
+    for hh in (ring(h + 1), ring(h - 1)):
+        peers += [at_img(x, hh, d), at_img(x, hh, o)]
+    for peer in peers:
+        pl.semaphore_signal(barrier, inc=1, device_id=peer, device_id_type=MESH)
+    pl.semaphore_wait(barrier, len(peers))
+    lane = lax.broadcasted_iota(jnp.int32, (1, 128), 1)
+
+    def noise_row(tile, count):
+        return jnp.concatenate([noise_ref[pl.ds(tile + t, 1), :] for t in range(count)], axis=1)
+
+
+    group_sum = jnp.concatenate([gsum_ref[...], jnp.zeros((GROUPS, 80), F32)], axis=1)
     other = at_img(x, h, o)
     rest_out[0:48, :] = jnp.dot(wts[...], shrest[o], preferred_element_type=F32).astype(BF16)
     rest_out[48:64, :] = group_sum.astype(BF16)
@@ -586,13 +582,6 @@
     )
     con_ref[...] = contrast
 
-    for e in range(4):
-        forward(columns[e], False)
-        for way in range(2):
-            y_copy(way, e, y).wait_send()
-            f_copy(way, e, y).wait_send()
-    for c in st_copies:
-        c.wait_send()
     for i in range(4):
         core_copy(i).wait_send()
     for c in (rest_copy, near_a, near_b, relay_up, relay_down, core_last):
@@ -610,15 +599,19 @@
     rows = jnp.pad(images.transpose(1, 0, 2).reshape(2 * NIMG, 264), ((0, 0), (0, 120)))
     vmem = pl.BlockSpec(memory_space=pltpu.VMEM)
     sem = pltpu.SemaphoreType.DMA
-    cls, con, ev = pl.pallas_call(
-        body,
+    noise = noise_weight.reshape(NPIX // 128, 128)
+    S = jax.ShapeDtypeStruct
+    smain, shrest, wts, gsum, ev = pl.pallas_call(
+        gather,
         out_shape=(
-            jax.ShapeDtypeStruct((2, NPROJ, 256), F32),
-            jax.ShapeDtypeStruct((NPROJ, 256), F32),
-            jax.ShapeDtypeStruct((1, 128), F32),
+            S((16, 2, ROWS, 256), BF16),
+            S((2, ROWS, 128), BF16),
+            S((NPROJ, ROWS), BF16),
+            S((GROUPS, NPROJ), F32),
+            S((1, 128), F32),
         ),
         in_specs=[vmem, vmem, vmem, vmem, vmem, pl.BlockSpec(memory_space=pltpu.SMEM), vmem, vmem],
-        out_specs=(vmem, vmem, vmem),
+        out_specs=(vmem,) * 5,
         scratch_shapes=[
             pltpu.VMEM((16, SHARD, 128), BF16),
             pltpu.VMEM((16, 2, NPROJ, 256), BF16),
@@ -627,11 +620,37 @@
             pltpu.VMEM((16, 8, 256), F32),
             pltpu.VMEM((8, 128), F32),
             pltpu.VMEM((8, 128), F32),
-            pltpu.VMEM((16, 2, ROWS, 256), BF16),
-            pltpu.VMEM((2, ROWS, 128), BF16),
             pltpu.VMEM((ROWS, NPROJ), F32),
-            pltpu.VMEM((NPROJ, ROWS), BF16),
             pltpu.VMEM((16, 8, 128), F32),
+            sem((4, 2)),
+            sem((4, 2)),
+            sem((2, 4, 2)),
+            sem((2, 4, 2)),
+            sem((2, 4)),
+            sem((2, 4)),
+            sem((16,)),
+            sem((16,)),
+        ],
+        compiler_params=pltpu.CompilerParams(
+            collective_id=0, has_side_effects=True, vmem_limit_bytes=30 * 1024 * 1024
+        ),
+        name="gather",
+    )(
+        rows,
+        projections.transpose(1, 0, 2),
+        contrast_curve,
+        noise,
+        defocus_group.reshape(1, NIMG),
+        shifts.T,
+        orient_index.reshape(1, NPROJ),
+        orient_prior.reshape(2, 128),
+    )
+    cls, con = pl.pallas_call(
+        reduce,
+        out_shape=(S((2, NPROJ, 256), F32), S((NPROJ, 256), F32)),
+        in_specs=[vmem] * 6,
+        out_specs=(vmem,) * 2,
+        scratch_shapes=[
             pltpu.VMEM((4, 8 * PIECE, 128), BF16),
             pltpu.VMEM((4, 8 * PIECE, 128), BF16),
             pltpu.VMEM((64, 128), BF16),
@@ -645,15 +664,6 @@
             pltpu.VMEM((2, 64, 128), BF16),
             pltpu.VMEM((2, 2, 64, 128), BF16),
             pltpu.VMEM((64, 128), BF16),
-            sem((4,)),
-            sem((4,)),
-            sem((4,)),
-            sem((2, 4)),
-            sem((2, 4)),
-            sem((2, 4)),
-            sem((2, 4)),
-            sem((16,)),
-            sem((16,)),
             sem((5,)),
             sem((5,)),
             sem((6,)),
@@ -662,19 +672,10 @@
             sem((7,)),
         ],
         compiler_params=pltpu.CompilerParams(
-            collective_id=0, has_side_effects=True, vmem_limit_bytes=40 * 1024 * 1024
+            collective_id=1, has_side_effects=True, vmem_limit_bytes=30 * 1024 * 1024
         ),
-        name="expectation",
-    )(
-        rows,
-        projections.transpose(1, 0, 2),
-        contrast_curve,
-        noise_weight.reshape(NPIX // 128, 128),
-        defocus_group.reshape(1, NIMG),
-        shifts.T,
-        orient_index.reshape(1, NPROJ),
-        orient_prior.reshape(2, 128),
-    )
+        name="reduce",
+    )(smain, shrest, wts, gsum, contrast_curve, noise)
     return cls[:, :, :132].transpose(1, 0, 2), con[:, :132], ev[0, :NIMG]
 
 

time: 66.5 us -> 70.5 us (1.060)
  local copies, waits for them, and re-layouts: 4.69 us -> 8.35 us
    unnamed x15, local copies, waits for them, and re-layouts: 3.25 us -> 6.9 us
    pallas_call x1 -> x2, Pallas kernels: 60.8 us -> 61.2 us  [the longest x1 32.7 us: on_device(): pl.pallas_call(reduce, out_shape=(S((2, NPROJ, 256), F32), S((NPROJ, 256)...]
where the time goes in v2:
time: 70.5 us; the launch traced here: 70.2 us
  Pallas kernels  61.2 us (87%)
  local copies, waits for them, and re-layouts  8.35 us (12%)
    pallas_call x1, Pallas kernels, on_device(): pl.pallas_call(reduce, out_shape=(S((2, NPROJ, 256), F32), S((NPROJ, 256)...  32.7 us
    pallas_call x1, Pallas kernels, on_device(): pl.pallas_call(gather, out_shape=(S((16, 2, ROWS, 256), BF16), S((2, ROWS...  28.5 us
    unnamed x15, local copies, waits for them, and re-layouts  6.9 us

profile of v2, /device:TPU:1, one launch (start us, length us, event | category | flops | bytes accessed | tf_op | source)
XLA Modules:
  0.0 70.2 jit_solution(5414947701136823774)
XLA Ops:
  0.6 0.9 %copy.11 = bf16[2,64,264]{2,1,0:T(8,128)(2,1)S(1)} copy(bf16[2,64,264]{2,0,1:T(2,128)(2,1)} %bitcast.24) | data formatting | bytes 135168 | tf_op jit(solution)/shard_map/transpose | solution.py:599
  1.6 1.2 %copy.15 = bf16[48,2,4224]{2,0,1:T(8,128)(2,1)S(1)} copy(bf16[48,2,4224]{2,1,0:T(2,128)(2,1)} %param.9) | data formatting | bytes 1622016 | tf_op args[1]
  2.8 0.0 copy-start
  2.8 0.9 %copy-done = f32[16,4224]{1,0:T(8,128)S(1)} copy-done((f32[16,4224]{1,0:T(8,128)S(1)}, f32[16,4224]{1,0:T(8,128)}, u32[]{:S(2)}) %copy-start) | copy-done | bytes 270360
  3.7 0.0 copy-start.1
  3.7 0.7 %copy-done.1 = f32[4224]{0:T(1024)S(1)} copy-done((f32[4224]{0:T(1024)S(1)}, f32[4224]{0:T(1024)}, u32[]{:S(2)}) %copy-start.1) | copy-done | bytes 16920
  4.5 0.0 copy-start.2
  4.5 0.7 copy-done.2
  5.2 0.0 copy-start.3
  5.2 0.7 copy-done.3
  5.8 0.0 copy-start.4
  5.8 0.7 copy-done.4
  6.5 0.0 copy-start.5
  6.5 0.7 copy-done.5
  7.1 28.5 %gather.1 = (bf16[16,2,576,256]{3,2,1,0:T(8,128)(2,1)S(1)}, bf16[2,576,128]{2,1,0:T(8,128)(2,1)S(1)}, bf16[48,576]{1,0:T(8,128)(2,1)S(1)}, f32[16,48]{1,0:T(8,128)S(1)}, f32[1,128]{1,0:T(1,128)S(1)}) custom-call(bf16[128,384]{1,0:T(8,128)(2,1)S(1)} %pad.4.img_ref, bf16[2,48,4224]{2,1,0:T(8,128)(2,1)S(1)} %bitcast.15, f32[16,4224]{1,0:T(8,128)S(1)} %copy-done, ...), custom_call_target="tpu_custom_call" | custom-call | tf_op jit(solution)/shard_map/gather/pallas_call | solution.py:604
  35.6 32.7 %reduce.1 = (f32[2,48,256]{2,1,0:T(8,128)S(1)}, f32[48,256]{1,0:T(8,128)S(1)}) custom-call(bf16[16,2,576,256]{3,2,1,0:T(8,128)(2,1)S(1)} %get-tuple-element.10.smain, bf16[2,576,128]{2,1,0:T(8,128)(2,1)S(1)} %get-tuple-element.11.shrest, bf16[48,576]{1,0:T(8,128)(2,1)S(1)} %get-tuple-element.12.wts, f32[16,48]{1,0:T(8,128)S(1)} %get-tuple-element.13.gsum_ref, ...), custom_call_target="tpu_custom_call" | custom-call | tf_op jit(solution)/shard_map/reduce/pallas_call | solution.py:648
  68.3 0.7 %copy.13 = f32[48,2,132]{2,1,0:T(2,128)} copy(f32[48,2,132]{2,0,1:T(8,128)S(1)} %slice_bitcast_fusion) | data formatting | bytes 101376
  69.1 0.5 slice_bitcast_fusion.1
  69.6 0.6 copy.17
  (2 shorter events, 0.0 us)
Async XLA Ops:
  2.8 1.0 %copy-start = (f32[16,4224]{1,0:T(8,128)S(1)}, f32[16,4224]{1,0:T(8,128)}, u32[]{:S(2)}) copy-start(f32[16,4224]{1,0:T(8,128)} %curve_ref.3) | copy-start | bytes 811012
  3.7 0.7 %copy-start.1 = (f32[4224]{0:T(1024)S(1)}, f32[4224]{0:T(1024)}, u32[]{:S(2)}) copy-start(f32[4224]{0:T(1024)} %param.11) | copy-start | bytes 50692
  4.5 0.7 copy-start.2
  5.2 0.7 copy-start.3
  5.8 0.7 copy-start.4
  6.5 0.7 copy-start.5

commit v3 on v1

--- a/solution.py
+++ b/solution.py
@@ -83,8 +83,7 @@
     z_relay,
     z_in,
     z_core,
-    ag_u_s,
-    ag_d_s,
+    ag_z_s,
     ag_z_r,
     ag_y_s,
     ag_y_r,
@@ -123,7 +122,8 @@
         )
 
     barrier = pltpu.get_barrier_semaphore()
-    peers = [dev(ref_at=lax.rem(ref + k, 16)) for k in range(1, 16)]
+    peers = [dev(ref_at=y * 4 + lax.rem(l + k, 4)) for k in range(1, 4)]
+    peers += [dev(ref_at=lax.rem(ref + 4 * k, 16)) for k in range(1, 4)]
     peers += [at_img(x, h, o), at_img(ring(x + 1), h, d), at_img(ring(x - 1), h, d)]
     for hh in (ring(h + 1), ring(h - 1)):
         peers += [at_img(x, hh, d), at_img(x, hh, o)]
@@ -161,58 +161,56 @@
 
     pl.semaphore_wait(barrier, len(peers))
 
-    col_1 = jnp.where(l == 0, 1, l - 1)
-    col_2 = jnp.where(l < 2, 2, jnp.where(l == 2, 3, 1))
-    col_3 = jnp.where(l < 2, 3, 0)
-    columns = [l, col_1, col_2, col_3]
+    columns = [lax.rem(l + 4 - e, 4) for e in range(4)]
+    halves = (pl.ds(0, 144), pl.ds(144, 128))
 
     def shard(yy, e):
         return yy * 4 + columns[e]
 
-    def z_copy_of(col, up):
-        block = xbuf.at[y * 4 + col]
-        to = dev(ref_at=y * 4 + lax.rem(l + (1 if up else 3), 4))
-        return copy(block, block, (ag_u_s if up else ag_d_s).at[col], ag_z_r.at[col], to)
-
-    def forward(col, start):
-        @pl.when((col <= l) & (l < 3))
-        def _():
-            c = z_copy_of(col, True)
-            c.start() if start else c.wait_send()
-
-        @pl.when((col >= l) & (l > 0))
-        def _():
-            c = z_copy_of(col, False)
-            c.start() if start else c.wait_send()
+    def z_send(e, part):
+        block = xbuf.at[ref, halves[part]]
+        to = dev(ref_at=y * 4 + lax.rem(l + e, 4))
+        return copy(block, block, ag_z_s.at[e, part], ag_z_r.at[e, part], to)
 
     y_up, y_down, y_far = ring(y + 1), ring(y - 1), ring(y + 2)
 
-    def y_copy(way, e, src_y):
+    def y_copy(way, e, src_y, part):
         to = dev(ref_at=(y_up if way == 0 else y_down) * 4 + l)
-        block = xbuf.at[shard(src_y, e)]
-        return copy(block, block, ag_y_s.at[way, e], ag_y_r.at[way, e], to)
+        block = xbuf.at[shard(src_y, e), halves[part]]
+        return copy(block, block, ag_y_s.at[way, e, part], ag_y_r.at[way, e, part], to)
 
     def f_copy(way, e, src_y):
         to = dev(ref_at=(y_up if way == 0 else y_down) * 4 + l)
-        rows = pl.ds(0, 144) if way == 0 else pl.ds(144, 128)
-        block = xbuf.at[shard(src_y, e), rows]
+        block = xbuf.at[shard(src_y, e), halves[way]]
         return copy(block, block, ag_f_s.at[way, e], ag_f_r.at[way, e], to)
 
-    y_copy(0, 0, y).start()
-    y_copy(1, 0, y).start()
-    forward(l, True)
+    def send_y(e):
+        y_copy(0, e, y, 0).start()
+        y_copy(1, e, y, 1).start()
+        y_copy(0, e, y, 1).start()
+        y_copy(1, e, y, 0).start()
+
+    z_send(1, 0).start()
+    z_send(3, 0).start()
+    send_y(0)
+    z_send(1, 1).start()
+    z_send(3, 1).start()
+    z_send(2, 0).start()
+    z_send(2, 1).start()
 
     def take_z(e):
-        z_copy_of(columns[e], True).wait_recv()
-        forward(columns[e], True)
-        y_copy(0, e, y).start()
-        y_copy(1, e, y).start()
+        for part in range(2):
+            block = xbuf.at[shard(y, e), halves[part]]
+            copy(block, block, ag_z_s.at[e, part], ag_z_r.at[e, part], dev(ref_at=shard(y, e))).wait_recv()
+        send_y(e)
 
     def take_y(e):
-        y_copy(0, e, y_down).wait_recv()
+        y_copy(0, e, y_down, 0).wait_recv()
         f_copy(0, e, y_down).start()
-        y_copy(1, e, y_up).wait_recv()
+        y_copy(1, e, y_up, 1).wait_recv()
         f_copy(1, e, y_up).start()
+        y_copy(0, e, y_down, 1).wait_recv()
+        y_copy(1, e, y_up, 0).wait_recv()
 
     def take_far(e):
         f_copy(0, e, y_far).wait_recv()
@@ -261,8 +259,9 @@
     for c in range(2):
         prest[c] = rests[c].astype(BF16)
 
+    take_y(0)
     take_z(1)
-    take_y(0)
+    take_z(3)
 
     def norm_step(t, total):
         span = pl.ds(pl.multiple_of(t * 384, 128), 384)
@@ -296,8 +295,6 @@
     base = prior - penalty
 
     score[...] = jnp.zeros_like(score)
-    take_z(2)
-    take_y(1)
 
     def process(b):
         for t in range(2):
@@ -328,19 +325,21 @@
 
         lax.fori_loop(0, len(blocks), step, 0)
 
-    process_all([shard(y, 0), shard(y, 1), shard(y_down, 0), shard(y_up, 0)])
-    take_z(3)
+    process(shard(y, 0))
+    take_z(2)
+    take_y(1)
+    process_all([shard(y, 1), shard(y_down, 0), shard(y_up, 0)])
+    take_y(3)
+    take_far(0)
+    process_all([shard(y, 3), shard(y_down, 1), shard(y_up, 1), shard(y_far, 0)])
     take_y(2)
-    take_far(0)
-    process_all([shard(y, 2), shard(y_down, 1), shard(y_up, 1), shard(y_far, 0)])
-    take_y(3)
     take_far(1)
-    process_all([shard(y, 3), shard(y_down, 2), shard(y_up, 2), shard(y_far, 1)])
-    process_all([shard(y_down, 3), shard(y_up, 3)])
+    process_all([shard(y, 2), shard(y_down, 3), shard(y_up, 3), shard(y_far, 1)])
+    process_all([shard(y_down, 2), shard(y_up, 2)])
+    take_far(3)
+    process(shard(y_far, 3))
     take_far(2)
     process(shard(y_far, 2))
-    take_far(3)
-    process(shard(y_far, 3))
 
     rest_t = jnp.concatenate([xbuf[b, 256:272, :].astype(F32)[:8] for b in range(16)], axis=0)
     rest_x = jnp.transpose(rest_t)
@@ -378,24 +377,35 @@
     total = jnp.sum(total, axis=0, keepdims=True)
     total = total + pltpu.roll(jnp.broadcast_to(total, (8, 128)), 64, 1)[:1]
     row8 = lax.broadcasted_iota(jnp.int32, (8, 128), 0)
-    stat[ref] = jnp.where(row8 == 0, high, total)
+
+    def merged(blocks):
+        top = blocks[0][0:1, :]
+        for block in blocks[1:]:
+            top = jnp.maximum(top, block[0:1, :])
+        whole = jnp.zeros((1, 128), F32)
+        for block in blocks:
+            whole += block[1:2, :] * jnp.exp(block[0:1, :] - top)
+        return top, whole
+
     st_copies = []
-    for k in range(1, 16):
-        st_copies.append(
-            copy(stat.at[ref], stat.at[ref], st_s.at[k], st_r.at[k], dev(ref_at=lax.rem(ref + k, 16)))
-        )
-    for c in st_copies:
-        c.start()
-    for k in range(1, 16):
-        src = lax.rem(ref + 16 - k, 16)
-        copy(stat.at[src], stat.at[src], st_s.at[k], st_r.at[k], dev(ref_at=src)).wait_recv()
-    highest = stat[0, 0:1, :]
-    for b in range(1, 16):
-        highest = jnp.maximum(highest, stat[b, 0:1, :])
-    whole = jnp.zeros((1, 128), F32)
-    for b in range(16):
-        whole += stat[b, 1:2, :] * jnp.exp(stat[b, 0:1, :] - highest)
-    evidence = highest + jnp.log(whole)
+    for stage in range(2):
+        mine_at = l if stage == 0 else y
+        stat[stage, mine_at] = jnp.where(row8 == 0, high, total)
+        for k in range(1, 4):
+            to = y * 4 + lax.rem(l + k, 4) if stage == 0 else lax.rem(ref + 4 * k, 16)
+            block = stat.at[stage, mine_at]
+            c = copy(block, block, st_s.at[3 * stage + k - 1], st_r.at[3 * stage + k - 1], dev(ref_at=to))
+            c.start()
+            st_copies.append(c)
+        for k in range(1, 4):
+            src = lax.rem(mine_at + 4 - k, 4)
+            block = stat.at[stage, src]
+            come_from = y * 4 + src if stage == 0 else src * 4 + l
+            copy(
+                block, block, st_s.at[3 * stage + k - 1], st_r.at[3 * stage + k - 1], dev(ref_at=come_from)
+            ).wait_recv()
+        high, total = merged([stat[stage, b] for b in range(4)])
+    evidence = high + jnp.log(total)
     ev_ref[...] = evidence
     for t in range(5):
         w = jnp.exp(tiles[t] - evidence).astype(BF16)
@@ -587,9 +597,12 @@
     con_ref[...] = contrast
 
     for e in range(4):
-        forward(columns[e], False)
+        for part in range(2):
+            if e:
+                z_send(e, part).wait_send()
+            for way in range(2):
+                y_copy(way, e, y, part).wait_send()
         for way in range(2):
-            y_copy(way, e, y).wait_send()
             f_copy(way, e, y).wait_send()
     for c in st_copies:
         c.wait_send()
@@ -631,7 +644,7 @@
             pltpu.VMEM((2, ROWS, 128), BF16),
             pltpu.VMEM((ROWS, NPROJ), F32),
             pltpu.VMEM((NPROJ, ROWS), BF16),
-            pltpu.VMEM((16, 8, 128), F32),
+            pltpu.VMEM((2, 4, 8, 128), F32),
             pltpu.VMEM((4, 8 * PIECE, 128), BF16),
             pltpu.VMEM((4, 8 * PIECE, 128), BF16),
             pltpu.VMEM((64, 128), BF16),
@@ -645,15 +658,14 @@
             pltpu.VMEM((2, 64, 128), BF16),
             pltpu.VMEM((2, 2, 64, 128), BF16),
             pltpu.VMEM((64, 128), BF16),
-            sem((4,)),
-            sem((4,)),
-            sem((4,)),
+            sem((4, 2)),
+            sem((4, 2)),
+            sem((2, 4, 2)),
+            sem((2, 4, 2)),
             sem((2, 4)),
             sem((2, 4)),
-            sem((2, 4)),
-            sem((2, 4)),
-            sem((16,)),
-            sem((16,)),
+            sem((6,)),
+            sem((6,)),
             sem((5,)),
             sem((5,)),
             sem((6,)),

time: 66.5 us -> 65.9 us (level)
  no operation moved by 1% of the time
where the time goes in v3:
time: 65.9 us; the launch traced here: 65.8 us
  Pallas kernels  60.3 us (92%)
  local copies, waits for them, and re-layouts  4.69 us (7%)
  between operations  0.74 us (1%)
    pallas_call x1, Pallas kernels, on_device(): pl.pallas_call(body, out_shape=(jax.ShapeDtypeStruct((2, NPROJ, 256), F32...  60.3 us
    unnamed x15, local copies, waits for them, and re-layouts  3.25 us

profile of v3, /device:TPU:1, one launch (start us, length us, event | category | flops | bytes accessed | tf_op | source)
XLA Modules:
  0.0 65.8 jit_solution(14988724226986619473)
XLA Ops:
  0.6 0.9 %copy.11 = bf16[2,64,264]{2,1,0:T(8,128)(2,1)S(1)} copy(bf16[2,64,264]{2,0,1:T(2,128)(2,1)} %bitcast.23) | data formatting | bytes 135168 | tf_op jit(solution)/shard_map/transpose | solution.py:623
  1.6 0.0 copy-start
  1.6 0.0 copy-start.1
  1.6 0.0 copy-start.3
  1.6 0.0 copy-start.5
  1.6 1.3 %copy.15 = bf16[48,2,4224]{2,0,1:T(8,128)(2,1)S(1)} copy(bf16[48,2,4224]{2,1,0:T(2,128)(2,1)} %param.9) | data formatting | bytes 1622016 | tf_op args[1]
  2.9 0.0 copy-start.2
  2.9 0.0 copy-start.4
  2.9 0.0 copy-done
  2.9 0.0 copy-done.1
  2.9 0.0 copy-done.3
  2.9 0.0 copy-done.5
  2.9 0.6 copy-done.2
  3.6 0.0 copy-done.4
  3.6 60.3 %expectation.1 = (f32[2,48,256]{2,1,0:T(8,128)S(1)}, f32[48,256]{1,0:T(8,128)S(1)}, f32[1,128]{1,0:T(1,128)S(1)}) custom-call(bf16[128,384]{1,0:T(8,128)(2,1)S(1)} %pad.4.img_ref, bf16[2,48,4224]{2,1,0:T(8,128)(2,1)S(1)} %bitcast.15, f32[16,4224]{1,0:T(8,128)S(1)} %copy-done, f32[33,128]{1,0:T(8,128)S(1)} %bitcast.17, s32[1,64]{1,0:T(1,128)S(1)} %bitcast.20, ...), custom_call_target="tpu_custom_call" | custom-call | tf_op jit(solution)/shard_map/expectation/pallas_call | solution.py:626
  63.9 0.7 %copy.13 = f32[48,2,132]{2,1,0:T(2,128)} copy(f32[48,2,132]{2,0,1:T(8,128)S(1)} %slice_bitcast_fusion) | data formatting | bytes 101376
  64.6 0.5 slice_bitcast_fusion.1
  65.1 0.6 copy.17
  (2 shorter events, 0.0 us)
Async XLA Ops:
  1.6 1.3 %copy-start = (f32[16,4224]{1,0:T(8,128)S(1)}, f32[16,4224]{1,0:T(8,128)}, u32[]{:S(2)}) copy-start(f32[16,4224]{1,0:T(8,128)} %curve_ref.1) | copy-start | bytes 811012
  1.6 1.3 %copy-start.1 = (f32[4224]{0:T(1024)S(1)}, f32[4224]{0:T(1024)}, u32[]{:S(2)}) copy-start(f32[4224]{0:T(1024)} %param.11) | copy-start | bytes 50692
  1.6 1.3 %copy-start.3 = (f32[256]{0:T(256)S(1)}, f32[256]{0:T(256)}, u32[]{:S(2)}) copy-start(f32[256]{0:T(256)} %param.15) | copy-start | bytes 3076
  1.6 1.3 %copy-start.5 = (s32[48]{0:T(128)S(1)}, s32[48]{0:T(128)}, u32[]{:S(2)}) copy-start(s32[48]{0:T(128)} %param.14) | copy-start | bytes 580
  2.9 0.7 %copy-start.2 = (s32[9,2]{0,1:T(2,128)S(1)}, s32[9,2]{0,1:T(2,128)}, u32[]{:S(2)}) copy-start(s32[9,2]{0,1:T(2,128)} %param.13) | copy-start | bytes 220
  2.9 0.7 %copy-start.4 = (s32[64]{0:T(128)S(1)}, s32[64]{0:T(128)}, u32[]{:S(2)}) copy-start(s32[64]{0:T(128)} %param.12) | copy-start | bytes 772

commit v4 on v3

--- a/solution.py
+++ b/solution.py
@@ -74,6 +74,7 @@
     core_in,
     rest_out,
     rest_in,
+    far_out,
     x_out,
     x_near_a,
     x_near_b,
@@ -125,6 +126,7 @@
     peers = [dev(ref_at=y * 4 + lax.rem(l + k, 4)) for k in range(1, 4)]
     peers += [dev(ref_at=lax.rem(ref + 4 * k, 16)) for k in range(1, 4)]
     peers += [at_img(x, h, o), at_img(ring(x + 1), h, d), at_img(ring(x - 1), h, d)]
+    peers += [at_img(ring(x + 1), h, o), at_img(ring(x - 1), h, o)]
     for hh in (ring(h + 1), ring(h - 1)):
         peers += [at_img(x, hh, d), at_img(x, hh, o)]
     for peer in peers:
@@ -184,15 +186,14 @@
         block = xbuf.at[shard(src_y, e), halves[way]]
         return copy(block, block, ag_f_s.at[way, e], ag_f_r.at[way, e], to)
 
-    def send_y(e):
-        y_copy(0, e, y, 0).start()
-        y_copy(1, e, y, 1).start()
-        y_copy(0, e, y, 1).start()
-        y_copy(1, e, y, 0).start()
+    def send_y(e, part):
+        for way in (part, 1 - part):
+            y_copy(way, e, y, part).start()
 
     z_send(1, 0).start()
     z_send(3, 0).start()
-    send_y(0)
+    send_y(0, 0)
+    send_y(0, 1)
     z_send(1, 1).start()
     z_send(3, 1).start()
     z_send(2, 0).start()
@@ -202,7 +203,7 @@
         for part in range(2):
             block = xbuf.at[shard(y, e), halves[part]]
             copy(block, block, ag_z_s.at[e, part], ag_z_r.at[e, part], dev(ref_at=shard(y, e))).wait_recv()
-        send_y(e)
+            send_y(e, part)
 
     def take_y(e):
         y_copy(0, e, y_down, 0).wait_recv()
@@ -418,10 +419,8 @@
     group_sum = jnp.concatenate([group_sum, jnp.zeros((GROUPS, 80), F32)], axis=1)
 
     other = at_img(x, h, o)
-    rest_out[0:48, :] = jnp.dot(wts[...], shrest[o], preferred_element_type=F32).astype(BF16)
-    rest_out[48:64, :] = group_sum.astype(BF16)
-    rest_copy = copy(rest_out, rest_in, co_s.at[4], co_r.at[4], other)
-    rest_copy.start()
+    rest_mine = jnp.dot(wts[...], shrest[d], preferred_element_type=F32)
+    rest_theirs = jnp.dot(wts[...], shrest[o], preferred_element_type=F32)
 
     order = [ring(x + 2), ring(x + 1), ring(x + 3), x]
     runs = [ring(h + 2), ring(h + 1), ring(h + 3), h]
@@ -437,79 +436,96 @@
                 core_out[i, r : r + PIECE, :] = got[:, v * 128 : v * 128 + 128].astype(BF16)
         core_copy(i).start()
 
-    other_chunk(0)
-    other_chunk(1)
-
-    rest_sum = jnp.dot(wts[...], shrest[d], preferred_element_type=F32)
-    rest_copy.wait_recv()
-    rest_sum = rest_sum + rest_in[0:48, :].astype(F32)
-    group_sum = group_sum + rest_in[48:64, :].astype(F32)
-
     def left(value, by):
         return pltpu.roll(value, lax.rem(256 - by, 128), 1)
 
-    group_half = left(group_sum, 32 + 24 * d)
-
-    def packed(q):
-        out = left(rest_sum[0:16], 32 * q)
-        out = jnp.where(lane < 32, out, left(rest_sum[16:32], 32 * q - 32))
-        out = jnp.where(lane < 64, out, left(rest_sum[32:48], 32 * q - 64))
-        return jnp.where(lane < 96, out, group_half)
+    def packed(q, rest_tile, group_tile, c):
+        out = left(rest_tile[0:16], 32 * q)
+        out = jnp.where(lane < 32, out, left(rest_tile[16:32], 32 * q - 32))
+        out = jnp.where(lane < 64, out, left(rest_tile[32:48], 32 * q - 64))
+        return jnp.where(lane < 96, out, left(group_tile, 32 + 24 * c))
 
     def piece_row(k):
         return 16 + PIECE * k
 
-    def own_chunk(i, store):
+    def rows_of(k):
+        return slice(0, 16) if k < 0 else slice(piece_row(k), piece_row(k) + PIECE)
+
+    far_copies = []
+    for k in range(2):
+        c = d if k == 0 else o
+        for u in range(4):
+            got = jnp.dot(wts[...], smain[4 * order[0] + runs[u], c], preferred_element_type=F32).astype(BF16)
+            for v in range(2):
+                far_out[k, rows_of(2 * u + v), :] = got[:, v * 128 : v * 128 + 128]
+        rest_tile = rest_mine if k == 0 else rest_theirs
+        far_out[k, 0:16, :] = packed(order[0], rest_tile, group_sum, c).astype(BF16)
+        for way in range(2):
+            rows = pl.ds(0, HALF) if way == 0 else pl.ds(HALF, MSG - HALF)
+            land = x_near_a if way == 0 else x_near_b
+            to = at_img(ring(x + 1) if way == 0 else ring(x - 1), h, c)
+            far_copies.append(
+                copy(far_out.at[k, rows], land.at[k], xs_s.at[2 * way + k], xs_r.at[2 * way + k], to)
+            )
+            far_copies[-1].start()
+
+    rest_out[0:48, :] = rest_theirs.astype(BF16)
+    rest_out[48:64, :] = group_sum.astype(BF16)
+    rest_copy = copy(rest_out, rest_in, co_s.at[4], co_r.at[4], other)
+    rest_copy.start()
+    for i in range(1, 4):
+        other_chunk(i)
+
+    rest_copy.wait_recv()
+    rest_sum = rest_mine + rest_in[0:48, :].astype(F32)
+    group_sum = group_sum + rest_in[48:64, :].astype(F32)
+
+    def own_chunk(i):
         q = order[i]
+        sums = [
+            jnp.dot(wts[...], smain[4 * q + runs[u], d], preferred_element_type=F32) for u in range(4)
+        ]
         core_copy(i).wait_recv()
         for u in range(4):
-            got = jnp.dot(wts[...], smain[4 * q + runs[u], d], preferred_element_type=F32)
             for v in range(2):
                 k = 2 * u + v
                 r = PIECE * k
-                store(k, got[:, v * 128 : v * 128 + 128] + core_in[i, r : r + PIECE, :].astype(F32))
-        store(-1, packed(q))
+                held[rows_of(k), :] = (
+                    sums[u][:, v * 128 : v * 128 + 128] + core_in[i, r : r + PIECE, :].astype(F32)
+                )
+        held[0:16, :] = packed(q, rest_sum, group_sum, d)
 
     x_up, x_down = at_img(ring(x + 1), h, d), at_img(ring(x - 1), h, d)
 
-    def rows_of(k):
-        return slice(0, 16) if k < 0 else slice(piece_row(k), piece_row(k) + PIECE)
-
-    def store_far(k, value):
-        x_out[0, rows_of(k), :] = value.astype(BF16)
-
-    own_chunk(0, store_far)
-    near_a = copy(x_out.at[0, pl.ds(0, HALF)], x_near_a, xs_s.at[0], xs_r.at[0], x_up)
-    near_b = copy(x_out.at[0, pl.ds(HALF, MSG - HALF)], x_near_b, xs_s.at[1], xs_r.at[1], x_down)
-    near_a.start()
-    near_b.start()
-
-    def store_up(k, value):
-        held[rows_of(k), :] = value
+    def near_wait(way):
+        for k in range(2):
+            far_copies[2 * k + way].wait_recv()
 
     def x_copy(way, part):
         rows = pl.ds(0, FIRST) if part == 0 else pl.ds(FIRST, MSG - FIRST)
-        k = 2 + 2 * way + part
+        k = 4 + 2 * way + part
         to = x_up if way == 0 else x_down
-        return copy(x_out.at[1 + way, rows], x_in.at[way, rows], xs_s.at[k], xs_r.at[k], to)
-
-    other_chunk(2)
-    own_chunk(1, store_up)
-    x_out[1, HALF:MSG, :] = held[HALF:MSG, :].astype(BF16)
-    near_a.wait_recv()
-    x_out[1, 0:HALF, :] = (held[0:HALF, :] + x_near_a[...].astype(F32)).astype(BF16)
+        return copy(x_out.at[way, rows], x_in.at[way, rows], xs_s.at[k], xs_r.at[k], to)
+
+    own_chunk(1)
+    x_out[0, HALF:MSG, :] = held[HALF:MSG, :].astype(BF16)
+    near_wait(0)
+    x_out[0, 0:HALF, :] = (
+        held[0:HALF, :] + x_near_a[0].astype(F32) + x_near_a[1].astype(F32)
+    ).astype(BF16)
     x_copy(0, 0).start()
     x_copy(0, 1).start()
 
-    other_chunk(3)
-    own_chunk(2, store_up)
-    x_out[2, 0:HALF, :] = held[0:HALF, :].astype(BF16)
+    own_chunk(2)
+    x_out[1, 0:HALF, :] = held[0:HALF, :].astype(BF16)
     x_copy(1, 0).start()
-    near_b.wait_recv()
-    x_out[2, HALF:MSG, :] = (held[HALF:MSG, :] + x_near_b[...].astype(F32)).astype(BF16)
+    near_wait(1)
+    x_out[1, HALF:MSG, :] = (
+        held[HALF:MSG, :] + x_near_b[0].astype(F32) + x_near_b[1].astype(F32)
+    ).astype(BF16)
     x_copy(1, 1).start()
 
-    own_chunk(3, store_up)
+    own_chunk(3)
 
     def add_x(part):
         rows = slice(0, FIRST) if part == 0 else slice(FIRST, MSG)
@@ -606,9 +622,11 @@
             f_copy(way, e, y).wait_send()
     for c in st_copies:
         c.wait_send()
-    for i in range(4):
+    for i in range(1, 4):
         core_copy(i).wait_send()
-    for c in (rest_copy, near_a, near_b, relay_up, relay_down, core_last):
+    for c in far_copies:
+        c.wait_send()
+    for c in (rest_copy, relay_up, relay_down, core_last):
         c.wait_send()
     for way in range(2):
         for part in range(2):
@@ -649,9 +667,10 @@
             pltpu.VMEM((4, 8 * PIECE, 128), BF16),
             pltpu.VMEM((64, 128), BF16),
             pltpu.VMEM((64, 128), BF16),
-            pltpu.VMEM((3, MSG, 128), BF16),
-            pltpu.VMEM((HALF, 128), BF16),
-            pltpu.VMEM((MSG - HALF, 128), BF16),
+            pltpu.VMEM((2, MSG, 128), BF16),
+            pltpu.VMEM((2, MSG, 128), BF16),
+            pltpu.VMEM((2, HALF, 128), BF16),
+            pltpu.VMEM((2, MSG - HALF, 128), BF16),
             pltpu.VMEM((2, MSG, 128), BF16),
             pltpu.VMEM((MSG, 128), F32),
             pltpu.VMEM((7, 64, 128), BF16),
@@ -668,8 +687,8 @@
             sem((6,)),
             sem((5,)),
             sem((5,)),
-            sem((6,)),
-            sem((6,)),
+            sem((8,)),
+            sem((8,)),
             sem((7,)),
             sem((7,)),
         ],

time: 65.9 us -> 63.9 us (0.970)
  Pallas kernels: 60.3 us -> 58.3 us
    pallas_call x1, Pallas kernels: 60.3 us -> 58.3 us  [on_device(): pl.pallas_call(body, out_shape=(jax.ShapeDtypeStruct((2, NPROJ, 256), F32...]
where the time goes in v4:
time: 63.9 us; the launch traced here: 63.8 us
  Pallas kernels  58.3 us (91%)
  local copies, waits for them, and re-layouts  4.69 us (7%)
  between operations  0.74 us (1%)
    pallas_call x1, Pallas kernels, on_device(): pl.pallas_call(body, out_shape=(jax.ShapeDtypeStruct((2, NPROJ, 256), F32...  58.3 us
    unnamed x15, local copies, waits for them, and re-layouts  3.25 us

profile of v4, /device:TPU:1, one launch (start us, length us, event | category | flops | bytes accessed | tf_op | source)
XLA Modules:
  0.0 63.8 jit_solution(15451522949423701936)
XLA Ops:
  0.6 0.9 %copy.11 = bf16[2,64,264]{2,1,0:T(8,128)(2,1)S(1)} copy(bf16[2,64,264]{2,0,1:T(2,128)(2,1)} %bitcast.23) | data formatting | bytes 135168 | tf_op jit(solution)/shard_map/transpose | solution.py:641
  1.6 0.0 copy-start
  1.6 0.0 copy-start.1
  1.6 0.0 copy-start.3
  1.6 0.0 copy-start.5
  1.6 1.3 %copy.15 = bf16[48,2,4224]{2,0,1:T(8,128)(2,1)S(1)} copy(bf16[48,2,4224]{2,1,0:T(2,128)(2,1)} %param.9) | data formatting | bytes 1622016 | tf_op args[1]
  2.9 0.0 copy-start.2
  2.9 0.0 copy-start.4
  2.9 0.0 copy-done
  2.9 0.0 copy-done.1
  2.9 0.0 copy-done.3
  2.9 0.0 copy-done.5
  2.9 0.6 copy-done.2
  3.6 0.0 copy-done.4
  3.6 58.3 %expectation.1 = (f32[2,48,256]{2,1,0:T(8,128)S(1)}, f32[48,256]{1,0:T(8,128)S(1)}, f32[1,128]{1,0:T(1,128)S(1)}) custom-call(bf16[128,384]{1,0:T(8,128)(2,1)S(1)} %pad.4.img_ref, bf16[2,48,4224]{2,1,0:T(8,128)(2,1)S(1)} %bitcast.15, f32[16,4224]{1,0:T(8,128)S(1)} %copy-done, f32[33,128]{1,0:T(8,128)S(1)} %bitcast.17, s32[1,64]{1,0:T(1,128)S(1)} %bitcast.20, ...), custom_call_target="tpu_custom_call" | custom-call | tf_op jit(solution)/shard_map/expectation/pallas_call | solution.py:644
  61.9 0.7 %copy.13 = f32[48,2,132]{2,1,0:T(2,128)} copy(f32[48,2,132]{2,0,1:T(8,128)S(1)} %slice_bitcast_fusion) | data formatting | bytes 101376
  62.6 0.5 slice_bitcast_fusion.1
  63.1 0.6 copy.17
  (2 shorter events, 0.0 us)
Async XLA Ops:
  1.6 1.3 %copy-start = (f32[16,4224]{1,0:T(8,128)S(1)}, f32[16,4224]{1,0:T(8,128)}, u32[]{:S(2)}) copy-start(f32[16,4224]{1,0:T(8,128)} %curve_ref.1) | copy-start | bytes 811012
  1.6 1.3 %copy-start.1 = (f32[4224]{0:T(1024)S(1)}, f32[4224]{0:T(1024)}, u32[]{:S(2)}) copy-start(f32[4224]{0:T(1024)} %param.11) | copy-start | bytes 50692
  1.6 1.3 %copy-start.3 = (f32[256]{0:T(256)S(1)}, f32[256]{0:T(256)}, u32[]{:S(2)}) copy-start(f32[256]{0:T(256)} %param.15) | copy-start | bytes 3076
  1.6 1.3 %copy-start.5 = (s32[48]{0:T(128)S(1)}, s32[48]{0:T(128)}, u32[]{:S(2)}) copy-start(s32[48]{0:T(128)} %param.14) | copy-start | bytes 580
  2.9 0.7 %copy-start.2 = (s32[9,2]{0,1:T(2,128)S(1)}, s32[9,2]{0,1:T(2,128)}, u32[]{:S(2)}) copy-start(s32[9,2]{0,1:T(2,128)} %param.13) | copy-start | bytes 220
  2.9 0.7 %copy-start.4 = (s32[64]{0:T(128)S(1)}, s32[64]{0:T(128)}, u32[]{:S(2)}) copy-start(s32[64]{0:T(128)} %param.12) | copy-start | bytes 772

commit v5 on v4

--- a/solution.py
+++ b/solution.py
@@ -47,17 +47,26 @@
 
 
 def body(
+    img_hbm,
+    proj_hbm,
+    curve_hbm,
+    noise_hbm,
+    group_hbm,
+    shift_hbm,
+    orient_hbm,
+    prior_hbm,
+    cls_ref,
+    group_out,
+    gain_out,
+    ev_ref,
     img_ref,
-    proj_ref,
     curve_ref,
     noise_ref,
     group_ref,
     shift_ref,
+    proj_ref,
     orient_ref,
     prior_ref,
-    cls_ref,
-    con_ref,
-    ev_ref,
     xbuf,
     pmain,
     prest,
@@ -98,6 +107,7 @@
     xs_r,
     zs_s,
     zs_r,
+    in_s,
 ):
     img = lax.axis_index("img")
     ref = lax.axis_index("ref")
@@ -131,6 +141,26 @@
         peers += [at_img(x, hh, d), at_img(x, hh, o)]
     for peer in peers:
         pl.semaphore_signal(barrier, inc=1, device_id=peer, device_id_type=MESH)
+
+    loads = [
+        pltpu.make_async_copy(src, dst, in_s.at[k])
+        for k, (src, dst) in enumerate(
+            (
+                (group_hbm, group_ref),
+                (curve_hbm, curve_ref),
+                (noise_hbm, noise_ref),
+                (img_hbm, img_ref),
+                (shift_hbm, shift_ref),
+                (proj_hbm, proj_ref),
+                (orient_hbm, orient_ref),
+                (prior_hbm, prior_ref),
+            )
+        )
+    ]
+    for load in loads:
+        load.start()
+    for load in loads[:4]:
+        load.wait()
 
     lane = lax.broadcasted_iota(jnp.int32, (1, 128), 1)
 
@@ -152,7 +182,15 @@
         for g in range(GROUPS):
             gain = jnp.where(group_col == float(g), curve_here[g : g + 1, span], gain)
         gain = gain * noise_here[:, span]
-        parts.append(img_ref[:, span].astype(F32) * jnp.concatenate([gain, gain], axis=0))
+        both = []
+        for c in range(2):
+            if tile < 2:
+                pixels = img_ref[:, c, span].astype(F32)
+            else:
+                pixels = img_ref[:, c, 256:264].astype(F32)
+                pixels = jnp.concatenate([pixels, jnp.zeros((NIMG, 120), F32)], axis=1)
+            both.append(pixels * gain)
+        parts.append(jnp.concatenate(both, axis=0))
     second = pltpu.roll(jnp.concatenate(parts[1:], axis=1), 252, 1)[:, :128]
     rest = jnp.transpose(jnp.where(lane < 4, parts[1], parts[2]))[:16, :]
     row16 = lax.broadcasted_iota(jnp.int32, (16, 128), 0)
@@ -216,6 +254,8 @@
     def take_far(e):
         f_copy(0, e, y_far).wait_recv()
         f_copy(1, e, y_far).wait_recv()
+
+    loads[4].wait()
 
     def table(pixel, width):
         srow = lax.broadcasted_iota(jnp.int32, (8, width), 0) + 1
@@ -242,13 +282,16 @@
     crest[...] = cosine
     srest[...] = sine
 
+    for load in loads[5:]:
+        load.wait()
+
     def proj_step(b, carry):
         out = []
         for c in range(2):
             kept = carry[c]
             for u in range(2):
                 n = 2 * b + u
-                window = proj_ref[c, :, pl.ds(pl.multiple_of(n * 128, 128), 256)].astype(F32)
+                window = proj_ref[:, c, pl.ds(pl.multiple_of(n * 128, 128), 256)].astype(F32)
                 turned = pltpu.roll(window, lax.rem(256 - 4 * n, 256), 1)
                 pmain[b, c, :, u * 128 : u * 128 + 128] = turned[:, :128].astype(BF16)
                 kept = jnp.where(lax.shift_right_logical(lane, 2) == n, window[:, 128:], kept)
@@ -266,8 +309,8 @@
 
     def norm_step(t, total):
         span = pl.ds(pl.multiple_of(t * 384, 128), 384)
-        re = proj_ref[0, :, span].astype(F32)
-        im = proj_ref[1, :, span].astype(F32)
+        re = proj_ref[:, 0, span].astype(F32)
+        im = proj_ref[:, 1, span].astype(F32)
         curve = curve_ref[:, span]
         gain = 0.5 * (curve * curve * noise_row(3 * t, 3))
         power = re * re + im * im
@@ -294,6 +337,9 @@
             jnp.where(hit, prior_ref[half : half + 1, :], 0.0), axis=1, keepdims=True
         )
     base = prior - penalty
+    span = pl.ds(pl.multiple_of(img * 128, 128), 256)
+    curve = curve_ref[:, span]
+    gain_out[...] = pltpu.roll(curve * curve * noise_row(img, 2), lax.rem(256 - 4 * img, 256), 1)
 
     score[...] = jnp.zeros_like(score)
 
@@ -326,17 +372,17 @@
 
         lax.fori_loop(0, len(blocks), step, 0)
 
-    process(shard(y, 0))
     take_z(2)
+    process_all([shard(y, 0), shard(y, 1)])
     take_y(1)
-    process_all([shard(y, 1), shard(y_down, 0), shard(y_up, 0)])
+    process_all([shard(y_down, 0), shard(y_up, 0)])
+    take_far(0)
     take_y(3)
-    take_far(0)
-    process_all([shard(y, 3), shard(y_down, 1), shard(y_up, 1), shard(y_far, 0)])
+    process_all([shard(y_far, 0), shard(y, 3), shard(y_down, 1)])
     take_y(2)
+    process_all([shard(y_up, 1), shard(y, 2), shard(y_down, 3), shard(y_up, 3)])
     take_far(1)
-    process_all([shard(y, 2), shard(y_down, 3), shard(y_up, 3), shard(y_far, 1)])
-    process_all([shard(y_down, 2), shard(y_up, 2)])
+    process_all([shard(y_far, 1), shard(y_down, 2), shard(y_up, 2)])
     take_far(3)
     process(shard(y_far, 3))
     take_far(2)
@@ -598,19 +644,7 @@
         for a in range(3):
             cls_ref[c, 16 * a : 16 * a + 16, 128:256] = left(pack, 32 * a + 4 * local)
     group_all = jnp.where(lane < 24, left(packs[0], 96), left(packs[1], 72))
-    group_all = jnp.where(lane < 48, group_all, 0.0)
-    span = pl.ds(pl.multiple_of(img * 128, 128), 256)
-    turn = lax.rem(256 - 4 * img, 256)
-    curve = curve_ref[:, span]
-    gain = pltpu.roll(curve * curve * noise_row(img, 2), turn, 1)
-    contrast = lax.dot_general(
-        jnp.transpose(jnp.concatenate([group_all, jnp.zeros((112, 128), F32)], axis=0))[:NPROJ, :GROUPS],
-        gain,
-        (((1,), (0,)), ((), ())),
-        precision=HIGHEST,
-        preferred_element_type=F32,
-    )
-    con_ref[...] = contrast
+    group_out[...] = jnp.where(lane < 48, group_all, 0.0)
 
     for e in range(4):
         for part in range(2):
@@ -635,22 +669,53 @@
         z_copy(slot).wait_send()
 
 
+def finish(
+    cls_hbm, group_hbm, gain_hbm, ev_hbm, cls_out, con_out, ev_out, cls_ref, group_ref, gain_ref, ev_ref, in_s
+):
+    loads = [
+        pltpu.make_async_copy(src, dst, in_s.at[k])
+        for k, (src, dst) in enumerate(
+            ((cls_hbm, cls_ref), (group_hbm, group_ref), (gain_hbm, gain_ref), (ev_hbm, ev_ref))
+        )
+    ]
+    for load in loads:
+        load.start()
+    for load in loads:
+        load.wait()
+    for c in range(2):
+        cls_out[:, c, :] = cls_ref[c, :, 0:132]
+    column = jnp.transpose(jnp.concatenate([group_ref[...], jnp.zeros((112, 128), F32)], axis=0))
+    con_out[...] = jnp.dot(
+        column[:NPROJ, :GROUPS], gain_ref[...], precision=HIGHEST, preferred_element_type=F32
+    )[:, :132]
+    ev_out[...] = ev_ref[:, :NIMG]
+
+
 def on_device(
     images, projections, contrast_curve, noise_weight, defocus_group, shifts, orient_index, orient_prior
 ):
-    rows = jnp.pad(images.transpose(1, 0, 2).reshape(2 * NIMG, 264), ((0, 0), (0, 120)))
     vmem = pl.BlockSpec(memory_space=pltpu.VMEM)
     sem = pltpu.SemaphoreType.DMA
-    cls, con, ev = pl.pallas_call(
+    hbm = pl.BlockSpec(memory_space=pl.ANY)
+    held = pl.pallas_call(
         body,
         out_shape=(
             jax.ShapeDtypeStruct((2, NPROJ, 256), F32),
-            jax.ShapeDtypeStruct((NPROJ, 256), F32),
+            jax.ShapeDtypeStruct((GROUPS, 128), F32),
+            jax.ShapeDtypeStruct((GROUPS, 256), F32),
             jax.ShapeDtypeStruct((1, 128), F32),
         ),
-        in_specs=[vmem, vmem, vmem, vmem, vmem, pl.BlockSpec(memory_space=pltpu.SMEM), vmem, vmem],
-        out_specs=(vmem, vmem, vmem),
+        in_specs=[hbm] * 8,
+        out_specs=(vmem,) * 4,
         scratch_shapes=[
+            pltpu.VMEM((NIMG, 2, 264), BF16),
+            pltpu.VMEM((GROUPS, NPIX), F32),
+            pltpu.VMEM((NPIX // 128, 128), F32),
+            pltpu.VMEM((1, NIMG), jnp.int32),
+            pltpu.SMEM((2, NSHIFT), jnp.int32),
+            pltpu.VMEM((NPROJ, 2, NPIX), BF16),
+            pltpu.VMEM((1, NPROJ), jnp.int32),
+            pltpu.VMEM((2, 128), F32),
             pltpu.VMEM((16, SHARD, 128), BF16),
             pltpu.VMEM((16, 2, NPROJ, 256), BF16),
             pltpu.VMEM((2, NPROJ, 128), BF16),
@@ -691,14 +756,15 @@
             sem((8,)),
             sem((7,)),
             sem((7,)),
+            sem((8,)),
         ],
         compiler_params=pltpu.CompilerParams(
-            collective_id=0, has_side_effects=True, vmem_limit_bytes=40 * 1024 * 1024
+            collective_id=0, has_side_effects=True, vmem_limit_bytes=60 * 1024 * 1024
         ),
         name="expectation",
     )(
-        rows,
-        projections.transpose(1, 0, 2),
+        images,
+        projections,
         contrast_curve,
         noise_weight.reshape(NPIX // 128, 128),
         defocus_group.reshape(1, NIMG),
@@ -706,7 +772,26 @@
         orient_index.reshape(1, NPROJ),
         orient_prior.reshape(2, 128),
     )
-    return cls[:, :, :132].transpose(1, 0, 2), con[:, :132], ev[0, :NIMG]
+    cls, con, ev = pl.pallas_call(
+        finish,
+        out_shape=(
+            jax.ShapeDtypeStruct((NPROJ, 2, 132), F32),
+            jax.ShapeDtypeStruct((NPROJ, 132), F32),
+            jax.ShapeDtypeStruct((1, NIMG), F32),
+        ),
+        in_specs=[hbm] * 4,
+        out_specs=(vmem,) * 3,
+        scratch_shapes=[
+            pltpu.VMEM((2, NPROJ, 256), F32),
+            pltpu.VMEM((GROUPS, 128), F32),
+            pltpu.VMEM((GROUPS, 256), F32),
+            pltpu.VMEM((1, 128), F32),
+            sem((4,)),
+        ],
+        compiler_params=pltpu.CompilerParams(vmem_limit_bytes=60 * 1024 * 1024),
+        name="finish",
+    )(*held)
+    return cls, con, ev.reshape(NIMG)
 
 
 def solution(mesh):

time: 63.9 us -> 63 us (0.986)
  local copies, waits for them, and re-layouts: 4.69 us -> 0 us
  Pallas kernels: 58.3 us -> 62.2 us
    unnamed x15 -> x0, local copies, waits for them, and re-layouts: 3.25 us -> none
    pallas_call x1, Pallas kernels: 58.3 us -> 60.4 us  [on_device(): pl.pallas_call(body, out_shape=(jax.ShapeDtypeStruct((2, NPROJ, 256), F32...]
    pallas_call x0 -> x1, Pallas kernels: none -> 1.8 us  [on_device(): pl.pallas_call(finish, out_shape=(jax.ShapeDtypeStruct((NPROJ, 2, 132), F...]
    transpose x2 -> x0, local copies, waits for them, and re-layouts: 0.92 us -> none  [the longest x1 0.91 us: on_device(): images.transpose(1, 0, 2).reshape(2 * NIMG, 264)]
where the time goes in v5:
time: 63 us; the launch traced here: 62.9 us
  Pallas kernels  62.2 us (99%)
  between operations  0.64 us (1%)
    pallas_call x1, Pallas kernels, on_device(): pl.pallas_call(body, out_shape=(jax.ShapeDtypeStruct((2, NPROJ, 256), F32...  60.4 us
    pallas_call x1, Pallas kernels, on_device(): pl.pallas_call(finish, out_shape=(jax.ShapeDtypeStruct((NPROJ, 2, 132), F...  1.8 us

profile of v5, /device:TPU:1, one launch (start us, length us, event | category | flops | bytes accessed | tf_op | source)
XLA Modules:
  0.0 62.9 jit_solution(9555429023663561102)
XLA Ops:
  0.6 60.4 %expectation.1 = (f32[2,48,256]{2,1,0:T(8,128)}, f32[16,128]{1,0:T(8,128)}, f32[16,256]{1,0:T(8,128)}, f32[1,128]{1,0:T(1,128)}) custom-call(bf16[64,2,264]{2,1,0:T(2,128)(2,1)} %img_hbm.1, bf16[48,2,4224]{2,1,0:T(2,128)(2,1)} %proj_hbm.1, f32[16,4224]{1,0:T(8,128)} %curve_hbm.1, f32[33,128]{1,0:T(8,128)} %bitcast.6, s32[1,64]{1,0:T(1,128)} %bitcast.9, ...), custom_call_target="tpu_custom_call" | custom-call | tf_op jit(solution)/shard_map/expectation/pallas_call | solution.py:700
  61.1 1.8 %finish.1 = (f32[48,2,132]{2,1,0:T(2,128)}, f32[48,132]{1,0:T(8,128)}, f32[1,64]{1,0:T(1,128)}) custom-call(f32[2,48,256]{2,1,0:T(8,128)} %get-tuple-element.10.cls_hbm, f32[16,128]{1,0:T(8,128)} %get-tuple-element.11.group_hbm, f32[16,256]{1,0:T(8,128)} %get-tuple-element.12.gain_hbm, f32[1,128]{1,0:T(1,128)} %get-tuple-element.13.ev_hbm), custom_call_target="tpu_custom_call" | custom-call | tf_op jit(solution)/shard_map/finish/pallas_call | solution.py:775

commit v6 on v5

--- a/solution.py
+++ b/solution.py
@@ -65,6 +65,7 @@
     group_ref,
     shift_ref,
     proj_ref,
+    planes,
     orient_ref,
     prior_ref,
     xbuf,
@@ -234,14 +235,11 @@
     send_y(0, 1)
     z_send(1, 1).start()
     z_send(3, 1).start()
-    z_send(2, 0).start()
-    z_send(2, 1).start()
-
-    def take_z(e):
-        for part in range(2):
-            block = xbuf.at[shard(y, e), halves[part]]
-            copy(block, block, ag_z_s.at[e, part], ag_z_r.at[e, part], dev(ref_at=shard(y, e))).wait_recv()
-            send_y(e, part)
+
+    def take_z(e, part):
+        block = xbuf.at[shard(y, e), halves[part]]
+        copy(block, block, ag_z_s.at[e, part], ag_z_r.at[e, part], dev(ref_at=shard(y, e))).wait_recv()
+        send_y(e, part)
 
     def take_y(e):
         y_copy(0, e, y_down, 0).wait_recv()
@@ -282,8 +280,21 @@
     crest[...] = cosine
     srest[...] = sine
 
+    z_send(2, 0).start()
+    z_send(2, 1).start()
+
     for load in loads[5:]:
         load.wait()
+
+    def plane_step(t, carry):
+        span = pl.ds(pl.multiple_of(t * 384, 128), 384)
+        for c in range(2):
+            planes[c, :, span] = proj_ref[:, c, span]
+        return carry
+
+    lax.fori_loop(0, 11, plane_step, 0)
+    take_y(0)
+
 
     def proj_step(b, carry):
         out = []
@@ -291,7 +302,7 @@
             kept = carry[c]
             for u in range(2):
                 n = 2 * b + u
-                window = proj_ref[:, c, pl.ds(pl.multiple_of(n * 128, 128), 256)].astype(F32)
+                window = planes[c, :, pl.ds(pl.multiple_of(n * 128, 128), 256)].astype(F32)
                 turned = pltpu.roll(window, lax.rem(256 - 4 * n, 256), 1)
                 pmain[b, c, :, u * 128 : u * 128 + 128] = turned[:, :128].astype(BF16)
                 kept = jnp.where(lax.shift_right_logical(lane, 2) == n, window[:, 128:], kept)
@@ -299,18 +310,19 @@
         return tuple(out)
 
     zero_rest = jnp.zeros((NPROJ, 128), F32)
-    rests = lax.fori_loop(0, 16, proj_step, (zero_rest, zero_rest))
+    rests = lax.fori_loop(0, 8, proj_step, (zero_rest, zero_rest))
+    for part in range(2):
+        take_z(1, part)
+        take_z(3, part)
+    rests = lax.fori_loop(8, 16, proj_step, rests)
     for c in range(2):
         prest[c] = rests[c].astype(BF16)
 
-    take_y(0)
-    take_z(1)
-    take_z(3)
 
     def norm_step(t, total):
         span = pl.ds(pl.multiple_of(t * 384, 128), 384)
-        re = proj_ref[:, 0, span].astype(F32)
-        im = proj_ref[:, 1, span].astype(F32)
+        re = planes[0, :, span].astype(F32)
+        im = planes[1, :, span].astype(F32)
         curve = curve_ref[:, span]
         gain = 0.5 * (curve * curve * noise_row(3 * t, 3))
         power = re * re + im * im
@@ -372,7 +384,8 @@
 
         lax.fori_loop(0, len(blocks), step, 0)
 
-    take_z(2)
+    take_z(2, 0)
+    take_z(2, 1)
     process_all([shard(y, 0), shard(y, 1)])
     take_y(1)
     process_all([shard(y_down, 0), shard(y_up, 0)])
@@ -714,6 +727,7 @@
             pltpu.VMEM((1, NIMG), jnp.int32),
             pltpu.SMEM((2, NSHIFT), jnp.int32),
             pltpu.VMEM((NPROJ, 2, NPIX), BF16),
+            pltpu.VMEM((2, NPROJ, NPIX), BF16),
             pltpu.VMEM((1, NPROJ), jnp.int32),
             pltpu.VMEM((2, 128), F32),
             pltpu.VMEM((16, SHARD, 128), BF16),

time: 63 us -> 61.2 us (0.971)
  Pallas kernels: 62.2 us -> 60.4 us
    pallas_call x1, Pallas kernels: 60.4 us -> 58.6 us  [on_device(): pl.pallas_call(body, out_shape=(jax.ShapeDtypeStruct((2, NPROJ, 256), F32...]
where the time goes in v6:
time: 61.2 us; the launch traced here: 61 us
  Pallas kernels  60.4 us (99%)
  between operations  0.64 us (1%)
    pallas_call x1, Pallas kernels, on_device(): pl.pallas_call(body, out_shape=(jax.ShapeDtypeStruct((2, NPROJ, 256), F32...  58.6 us
    pallas_call x1, Pallas kernels, on_device(): pl.pallas_call(finish, out_shape=(jax.ShapeDtypeStruct((NPROJ, 2, 132), F...  1.8 us

profile of v6, /device:TPU:1, one launch (start us, length us, event | category | flops | bytes accessed | tf_op | source)
XLA Modules:
  0.0 61.0 jit_solution(2988286504385949834)
XLA Ops:
  0.6 58.6 %expectation.1 = (f32[2,48,256]{2,1,0:T(8,128)}, f32[16,128]{1,0:T(8,128)}, f32[16,256]{1,0:T(8,128)}, f32[1,128]{1,0:T(1,128)}) custom-call(bf16[64,2,264]{2,1,0:T(2,128)(2,1)} %img_hbm.1, bf16[48,2,4224]{2,1,0:T(2,128)(2,1)} %proj_hbm.1, f32[16,4224]{1,0:T(8,128)} %curve_hbm.1, f32[33,128]{1,0:T(8,128)} %bitcast.6, s32[1,64]{1,0:T(1,128)} %bitcast.9, ...), custom_call_target="tpu_custom_call" | custom-call | tf_op jit(solution)/shard_map/expectation/pallas_call | solution.py:713
  59.2 1.8 %finish.1 = (f32[48,2,132]{2,1,0:T(2,128)}, f32[48,132]{1,0:T(8,128)}, f32[1,64]{1,0:T(1,128)}) custom-call(f32[2,48,256]{2,1,0:T(8,128)} %get-tuple-element.10.cls_hbm, f32[16,128]{1,0:T(8,128)} %get-tuple-element.11.group_hbm, f32[16,256]{1,0:T(8,128)} %get-tuple-element.12.gain_hbm, f32[1,128]{1,0:T(1,128)} %get-tuple-element.13.ev_hbm), custom_call_target="tpu_custom_call" | custom-call | tf_op jit(solution)/shard_map/finish/pallas_call | solution.py:789

commit v7 on v6

--- a/solution.py
+++ b/solution.py
@@ -229,12 +229,17 @@
         for way in (part, 1 - part):
             y_copy(way, e, y, part).start()
 
-    z_send(1, 0).start()
-    z_send(3, 0).start()
+    def near_z():
+        for part in range(2):
+            z_send(1, part).start()
+            z_send(3, part).start()
+
+    @pl.when(d == 0)
+    def _():
+        near_z()
+
     send_y(0, 0)
     send_y(0, 1)
-    z_send(1, 1).start()
-    z_send(3, 1).start()
 
     def take_z(e, part):
         block = xbuf.at[shard(y, e), halves[part]]
@@ -280,8 +285,14 @@
     crest[...] = cosine
     srest[...] = sine
 
-    z_send(2, 0).start()
-    z_send(2, 1).start()
+    @pl.when(d == 1)
+    def _():
+        near_z()
+
+    @pl.when(d == 0)
+    def _():
+        for part in range(2):
+            z_send(2, part).start()
 
     for load in loads[5:]:
         load.wait()
@@ -293,6 +304,12 @@
         return carry
 
     lax.fori_loop(0, 11, plane_step, 0)
+
+    @pl.when(d == 1)
+    def _():
+        for part in range(2):
+            z_send(2, part).start()
+
     take_y(0)
 
 

time: 61.2 us -> 61.6 us (level)
  no operation moved by 1% of the time
where the time goes in v7:
time: 61.6 us; the launch traced here: 61.4 us
  Pallas kernels  60.8 us (99%)
  between operations  0.64 us (1%)
    pallas_call x1, Pallas kernels, on_device(): pl.pallas_call(body, out_shape=(jax.ShapeDtypeStruct((2, NPROJ, 256), F32...  59 us
    pallas_call x1, Pallas kernels, on_device(): pl.pallas_call(finish, out_shape=(jax.ShapeDtypeStruct((NPROJ, 2, 132), F...  1.8 us

profile of v7, /device:TPU:1, one launch (start us, length us, event | category | flops | bytes accessed | tf_op | source)
XLA Modules:
  0.0 61.4 jit_solution(14886107423975877851)
XLA Ops:
  0.6 59.0 %expectation.1 = (f32[2,48,256]{2,1,0:T(8,128)}, f32[16,128]{1,0:T(8,128)}, f32[16,256]{1,0:T(8,128)}, f32[1,128]{1,0:T(1,128)}) custom-call(bf16[64,2,264]{2,1,0:T(2,128)(2,1)} %img_hbm.1, bf16[48,2,4224]{2,1,0:T(2,128)(2,1)} %proj_hbm.1, f32[16,4224]{1,0:T(8,128)} %curve_hbm.1, f32[33,128]{1,0:T(8,128)} %bitcast.6, s32[1,64]{1,0:T(1,128)} %bitcast.9, ...), custom_call_target="tpu_custom_call" | custom-call | tf_op jit(solution)/shard_map/expectation/pallas_call | solution.py:730
  59.6 1.8 %finish.1 = (f32[48,2,132]{2,1,0:T(2,128)}, f32[48,132]{1,0:T(8,128)}, f32[1,64]{1,0:T(1,128)}) custom-call(f32[2,48,256]{2,1,0:T(8,128)} %get-tuple-element.10.cls_hbm, f32[16,128]{1,0:T(8,128)} %get-tuple-element.11.group_hbm, f32[16,256]{1,0:T(8,128)} %get-tuple-element.12.gain_hbm, f32[1,128]{1,0:T(1,128)} %get-tuple-element.13.ev_hbm), custom_call_target="tpu_custom_call" | custom-call | tf_op jit(solution)/shard_map/finish/pallas_call | solution.py:806

commit v8 on v7

--- a/solution.py
+++ b/solution.py
@@ -78,6 +78,7 @@
     smain,
     shrest,
     score,
+    tile_sum,
     wts,
     stat,
     core_out,
@@ -86,8 +87,7 @@
     rest_in,
     far_out,
     x_out,
-    x_near_a,
-    x_near_b,
+    x_near,
     x_in,
     held,
     z_out,
@@ -372,7 +372,7 @@
 
     score[...] = jnp.zeros_like(score)
 
-    def process(b):
+    def process(b, last=False):
         for t in range(2):
             span = slice(t * 128, t * 128 + 128)
             re = xbuf[b, t * 128 : t * 128 + 64, :]
@@ -387,6 +387,10 @@
                 sine = stab[b, s - 1 : s, span]
                 smain[b, 0, rows, span] = (re * cosine + im * sine).astype(BF16)
                 smain[b, 1, rows, span] = (im * cosine - re * sine).astype(BF16)
+        if last:
+            return lax.dot_general(
+                pmain[b, 0], smain[b, 0], NT, preferred_element_type=F32
+            ) + lax.dot_general(pmain[b, 1], smain[b, 1], NT, preferred_element_type=F32)
         score[...] += lax.dot_general(
             smain[b, 0], pmain[b, 0], NT, preferred_element_type=F32
         ) + lax.dot_general(smain[b, 1], pmain[b, 1], NT, preferred_element_type=F32)
@@ -415,8 +419,15 @@
     process_all([shard(y_far, 1), shard(y_down, 2), shard(y_up, 2)])
     take_far(3)
     process(shard(y_far, 3))
+    full = jnp.concatenate([score[...], jnp.zeros((ROWS, 128 - NPROJ), F32)], axis=1)
+    for t in range(5):
+        if t < 4:
+            turned = full[t * 128 : t * 128 + 128]
+        else:
+            turned = jnp.concatenate([full[512:576], jnp.zeros((64, 128), F32)], axis=0)
+        tile_sum[t] = jnp.transpose(turned)[:NPROJ] + base
     take_far(2)
-    process(shard(y_far, 2))
+    last_part = process(shard(y_far, 2), last=True)
 
     rest_t = jnp.concatenate([xbuf[b, 256:272, :].astype(F32)[:8] for b in range(16)], axis=0)
     rest_x = jnp.transpose(rest_t)
@@ -429,20 +440,16 @@
         sine = srest[s - 1 : s, :]
         shrest[0, rows, :] = (re * cosine + im * sine).astype(BF16)
         shrest[1, rows, :] = (im * cosine - re * sine).astype(BF16)
-    full = (
-        score[...]
-        + lax.dot_general(shrest[0], prest[0], NT, preferred_element_type=F32)
-        + lax.dot_general(shrest[1], prest[1], NT, preferred_element_type=F32)
-    )
-    full = jnp.concatenate([full, jnp.zeros((ROWS, 128 - NPROJ), F32)], axis=1)
-
+    last_part += lax.dot_general(
+        prest[0], shrest[0], NT, preferred_element_type=F32
+    ) + lax.dot_general(prest[1], shrest[1], NT, preferred_element_type=F32)
     tiles = []
     for t in range(5):
         if t < 4:
-            tiles.append(jnp.transpose(full[t * 128 : t * 128 + 128])[:NPROJ] + base)
+            tiles.append(tile_sum[t] + last_part[:, t * 128 : t * 128 + 128])
         else:
-            last = jnp.concatenate([full[512:576], jnp.zeros((64, 128), F32)], axis=0)
-            tiles.append(jnp.where(lane < 64, jnp.transpose(last)[:NPROJ] + base, -3e38))
+            end = jnp.concatenate([last_part[:, 512:576]] * 2, axis=1)
+            tiles.append(jnp.where(lane < 64, tile_sum[t] + end, -3e38))
     high = tiles[0]
     for t in range(1, 5):
         high = jnp.maximum(high, tiles[t])
@@ -527,23 +534,33 @@
     def rows_of(k):
         return slice(0, 16) if k < 0 else slice(piece_row(k), piece_row(k) + PIECE)
 
-    far_copies = []
-    for k in range(2):
+    far_spans = (slice(0, FIRST), slice(FIRST, HALF), slice(HALF, MSG))
+
+    def far_copy(k, part):
+        span = far_spans[part]
+        rows = pl.ds(span.start, span.stop - span.start)
         c = d if k == 0 else o
-        for u in range(4):
-            got = jnp.dot(wts[...], smain[4 * order[0] + runs[u], c], preferred_element_type=F32).astype(BF16)
+        to = at_img(ring(x + 1) if part < 2 else ring(x - 1), h, c)
+        at = 2 * part + k
+        return copy(far_out.at[k, rows], x_near.at[k, rows], xs_s.at[at], xs_r.at[at], to)
+
+    def far_sums(k, runs_of):
+        for u in runs_of:
+            got = jnp.dot(
+                wts[...], smain[4 * order[0] + runs[u], d if k == 0 else o], preferred_element_type=F32
+            ).astype(BF16)
             for v in range(2):
                 far_out[k, rows_of(2 * u + v), :] = got[:, v * 128 : v * 128 + 128]
+
+    for k in range(2):
+        far_sums(k, (0,))
         rest_tile = rest_mine if k == 0 else rest_theirs
-        far_out[k, 0:16, :] = packed(order[0], rest_tile, group_sum, c).astype(BF16)
-        for way in range(2):
-            rows = pl.ds(0, HALF) if way == 0 else pl.ds(HALF, MSG - HALF)
-            land = x_near_a if way == 0 else x_near_b
-            to = at_img(ring(x + 1) if way == 0 else ring(x - 1), h, c)
-            far_copies.append(
-                copy(far_out.at[k, rows], land.at[k], xs_s.at[2 * way + k], xs_r.at[2 * way + k], to)
-            )
-            far_copies[-1].start()
+        far_out[k, 0:16, :] = packed(order[0], rest_tile, group_sum, d if k == 0 else o).astype(BF16)
+        far_copy(k, 0).start()
+    for k in range(2):
+        far_sums(k, (1, 2, 3))
+        far_copy(k, 2).start()
+        far_copy(k, 1).start()
 
     rest_out[0:48, :] = rest_theirs.astype(BF16)
     rest_out[48:64, :] = group_sum.astype(BF16)
@@ -573,32 +590,30 @@
 
     x_up, x_down = at_img(ring(x + 1), h, d), at_img(ring(x - 1), h, d)
 
-    def near_wait(way):
+    def near_sum(part):
+        span = far_spans[part]
         for k in range(2):
-            far_copies[2 * k + way].wait_recv()
+            far_copy(k, part).wait_recv()
+        both = x_near[0, span, :].astype(F32) + x_near[1, span, :].astype(F32)
+        return (held[span, :] + both).astype(BF16)
 
     def x_copy(way, part):
         rows = pl.ds(0, FIRST) if part == 0 else pl.ds(FIRST, MSG - FIRST)
-        k = 4 + 2 * way + part
+        k = 6 + 2 * way + part
         to = x_up if way == 0 else x_down
         return copy(x_out.at[way, rows], x_in.at[way, rows], xs_s.at[k], xs_r.at[k], to)
 
     own_chunk(1)
+    x_out[0, 0:FIRST, :] = near_sum(0)
+    x_copy(0, 0).start()
     x_out[0, HALF:MSG, :] = held[HALF:MSG, :].astype(BF16)
-    near_wait(0)
-    x_out[0, 0:HALF, :] = (
-        held[0:HALF, :] + x_near_a[0].astype(F32) + x_near_a[1].astype(F32)
-    ).astype(BF16)
-    x_copy(0, 0).start()
+    x_out[0, FIRST:HALF, :] = near_sum(1)
     x_copy(0, 1).start()
 
     own_chunk(2)
     x_out[1, 0:HALF, :] = held[0:HALF, :].astype(BF16)
     x_copy(1, 0).start()
-    near_wait(1)
-    x_out[1, HALF:MSG, :] = (
-        held[HALF:MSG, :] + x_near_b[0].astype(F32) + x_near_b[1].astype(F32)
-    ).astype(BF16)
+    x_out[1, HALF:MSG, :] = near_sum(2)
     x_copy(1, 1).start()
 
     own_chunk(3)
@@ -688,8 +703,9 @@
         c.wait_send()
     for i in range(1, 4):
         core_copy(i).wait_send()
-    for c in far_copies:
-        c.wait_send()
+    for k in range(2):
+        for part in range(3):
+            far_copy(k, part).wait_send()
     for c in (rest_copy, relay_up, relay_down, core_last):
         c.wait_send()
     for way in range(2):
@@ -757,6 +773,7 @@
             pltpu.VMEM((16, 2, ROWS, 256), BF16),
             pltpu.VMEM((2, ROWS, 128), BF16),
             pltpu.VMEM((ROWS, NPROJ), F32),
+            pltpu.VMEM((5, NPROJ, 128), F32),
             pltpu.VMEM((NPROJ, ROWS), BF16),
             pltpu.VMEM((2, 4, 8, 128), F32),
             pltpu.VMEM((4, 8 * PIECE, 128), BF16),
@@ -765,8 +782,7 @@
             pltpu.VMEM((64, 128), BF16),
             pltpu.VMEM((2, MSG, 128), BF16),
             pltpu.VMEM((2, MSG, 128), BF16),
-            pltpu.VMEM((2, HALF, 128), BF16),
-            pltpu.VMEM((2, MSG - HALF, 128), BF16),
+            pltpu.VMEM((2, MSG, 128), BF16),
             pltpu.VMEM((2, MSG, 128), BF16),
             pltpu.VMEM((MSG, 128), F32),
             pltpu.VMEM((7, 64, 128), BF16),
@@ -783,8 +799,8 @@
             sem((6,)),
             sem((5,)),
             sem((5,)),
-            sem((8,)),
-            sem((8,)),
+            sem((10,)),
+            sem((10,)),
             sem((7,)),
             sem((7,)),
             sem((8,)),

time: 61.6 us -> 61.3 us (level); the launches traced: 61.4 us -> 60.2 us
  Pallas kernels: 60.8 us -> 59.6 us
    pallas_call x1, Pallas kernels: 59 us -> 57.8 us  [on_device(): pl.pallas_call(body, out_shape=(jax.ShapeDtypeStruct((2, NPROJ, 256), F32...]
where the time goes in v8:
time: 61.3 us; the launch traced here: 60.2 us
  Pallas kernels  59.6 us (97%)
  between operations  0.64 us (1%)
    pallas_call x1, Pallas kernels, on_device(): pl.pallas_call(body, out_shape=(jax.ShapeDtypeStruct((2, NPROJ, 256), F32...  57.8 us
    pallas_call x1, Pallas kernels, on_device(): pl.pallas_call(finish, out_shape=(jax.ShapeDtypeStruct((NPROJ, 2, 132), F...  1.8 us

profile of v8, /device:TPU:1, one launch (start us, length us, event | category | flops | bytes accessed | tf_op | source)
XLA Modules:
  0.0 60.2 jit_solution(620101774616912731)
XLA Ops:
  0.6 57.8 %expectation.1 = (f32[2,48,256]{2,1,0:T(8,128)}, f32[16,128]{1,0:T(8,128)}, f32[16,256]{1,0:T(8,128)}, f32[1,128]{1,0:T(1,128)}) custom-call(bf16[64,2,264]{2,1,0:T(2,128)(2,1)} %img_hbm.1, bf16[48,2,4224]{2,1,0:T(2,128)(2,1)} %proj_hbm.1, f32[16,4224]{1,0:T(8,128)} %curve_hbm.1, f32[33,128]{1,0:T(8,128)} %bitcast.6, s32[1,64]{1,0:T(1,128)} %bitcast.9, ...), custom_call_target="tpu_custom_call" | custom-call | tf_op jit(solution)/shard_map/expectation/pallas_call | solution.py:746
  58.4 1.8 %finish.1 = (f32[48,2,132]{2,1,0:T(2,128)}, f32[48,132]{1,0:T(8,128)}, f32[1,64]{1,0:T(1,128)}) custom-call(f32[2,48,256]{2,1,0:T(8,128)} %get-tuple-element.10.cls_hbm, f32[16,128]{1,0:T(8,128)} %get-tuple-element.11.group_hbm, f32[16,256]{1,0:T(8,128)} %get-tuple-element.12.gain_hbm, f32[1,128]{1,0:T(1,128)} %get-tuple-element.13.ev_hbm), custom_call_target="tpu_custom_call" | custom-call | tf_op jit(solution)/shard_map/finish/pallas_call | solution.py:822

commit v9 on v8

--- a/solution.py
+++ b/solution.py
@@ -202,11 +202,12 @@
 
     pl.semaphore_wait(barrier, len(peers))
 
-    columns = [lax.rem(l + 4 - e, 4) for e in range(4)]
+    near = jnp.where(l == 0, 3, 1)
+    next_near = 4 - near
     halves = (pl.ds(0, 144), pl.ds(144, 128))
 
     def shard(yy, e):
-        return yy * 4 + columns[e]
+        return yy * 4 + lax.rem(l + 4 - e, 4)
 
     def z_send(e, part):
         block = xbuf.at[ref, halves[part]]
@@ -310,6 +311,10 @@
         for part in range(2):
             z_send(2, part).start()
 
+    for part in range(2):
+        take_z(near, part)
+    for part in range(2):
+        take_z(next_near, part)
     take_y(0)
 
 
@@ -327,11 +332,7 @@
         return tuple(out)
 
     zero_rest = jnp.zeros((NPROJ, 128), F32)
-    rests = lax.fori_loop(0, 8, proj_step, (zero_rest, zero_rest))
-    for part in range(2):
-        take_z(1, part)
-        take_z(3, part)
-    rests = lax.fori_loop(8, 16, proj_step, rests)
+    rests = lax.fori_loop(0, 16, proj_step, (zero_rest, zero_rest))
     for c in range(2):
         prest[c] = rests[c].astype(BF16)
 
@@ -407,18 +408,18 @@
 
     take_z(2, 0)
     take_z(2, 1)
-    process_all([shard(y, 0), shard(y, 1)])
-    take_y(1)
+    process_all([shard(y, 0), shard(y, near)])
+    take_y(near)
     process_all([shard(y_down, 0), shard(y_up, 0)])
     take_far(0)
-    take_y(3)
-    process_all([shard(y_far, 0), shard(y, 3), shard(y_down, 1)])
+    take_y(next_near)
+    process_all([shard(y_far, 0), shard(y, next_near), shard(y_down, near)])
     take_y(2)
-    process_all([shard(y_up, 1), shard(y, 2), shard(y_down, 3), shard(y_up, 3)])
-    take_far(1)
-    process_all([shard(y_far, 1), shard(y_down, 2), shard(y_up, 2)])
-    take_far(3)
-    process(shard(y_far, 3))
+    process_all([shard(y_up, near), shard(y, 2), shard(y_down, next_near), shard(y_up, next_near)])
+    take_far(near)
+    process_all([shard(y_far, near), shard(y_down, 2), shard(y_up, 2)])
+    take_far(next_near)
+    process(shard(y_far, next_near))
     full = jnp.concatenate([score[...], jnp.zeros((ROWS, 128 - NPROJ), F32)], axis=1)
     for t in range(5):
         if t < 4:

time: 61.3 us -> 62.1 us (1.013)
  Pallas kernels: 59.6 us -> 60.7 us
    pallas_call x1, Pallas kernels: 57.8 us -> 58.9 us  [on_device(): pl.pallas_call(body, out_shape=(jax.ShapeDtypeStruct((2, NPROJ, 256), F32...]
where the time goes in v9:
time: 62.1 us; the launch traced here: 61.3 us
  Pallas kernels  60.7 us (98%)
  between operations  0.64 us (1%)
    pallas_call x1, Pallas kernels, on_device(): pl.pallas_call(body, out_shape=(jax.ShapeDtypeStruct((2, NPROJ, 256), F32...  58.9 us
    pallas_call x1, Pallas kernels, on_device(): pl.pallas_call(finish, out_shape=(jax.ShapeDtypeStruct((NPROJ, 2, 132), F...  1.8 us

profile of v9, /device:TPU:1, one launch (start us, length us, event | category | flops | bytes accessed | tf_op | source)
XLA Modules:
  0.0 61.3 jit_solution(3877973485927894698)
XLA Ops:
  0.6 58.9 %expectation.1 = (f32[2,48,256]{2,1,0:T(8,128)}, f32[16,128]{1,0:T(8,128)}, f32[16,256]{1,0:T(8,128)}, f32[1,128]{1,0:T(1,128)}) custom-call(bf16[64,2,264]{2,1,0:T(2,128)(2,1)} %img_hbm.1, bf16[48,2,4224]{2,1,0:T(2,128)(2,1)} %proj_hbm.1, f32[16,4224]{1,0:T(8,128)} %curve_hbm.1, f32[33,128]{1,0:T(8,128)} %bitcast.6, s32[1,64]{1,0:T(1,128)} %bitcast.9, ...), custom_call_target="tpu_custom_call" | custom-call | tf_op jit(solution)/shard_map/expectation/pallas_call | solution.py:747
  59.5 1.8 %finish.1 = (f32[48,2,132]{2,1,0:T(2,128)}, f32[48,132]{1,0:T(8,128)}, f32[1,64]{1,0:T(1,128)}) custom-call(f32[2,48,256]{2,1,0:T(8,128)} %get-tuple-element.10.cls_hbm, f32[16,128]{1,0:T(8,128)} %get-tuple-element.11.group_hbm, f32[16,256]{1,0:T(8,128)} %get-tuple-element.12.gain_hbm, f32[1,128]{1,0:T(1,128)} %get-tuple-element.13.ev_hbm), custom_call_target="tpu_custom_call" | custom-call | tf_op jit(solution)/shard_map/finish/pallas_call | solution.py:823

commit v10 on v8

--- a/solution.py
+++ b/solution.py
@@ -336,40 +336,6 @@
         prest[c] = rests[c].astype(BF16)
 
 
-    def norm_step(t, total):
-        span = pl.ds(pl.multiple_of(t * 384, 128), 384)
-        re = planes[0, :, span].astype(F32)
-        im = planes[1, :, span].astype(F32)
-        curve = curve_ref[:, span]
-        gain = 0.5 * (curve * curve * noise_row(3 * t, 3))
-        power = re * re + im * im
-        return total + lax.dot_general(
-            two_parts(power), two_parts(gain), NT, preferred_element_type=F32
-        )
-
-    def two_parts(value):
-        high = value.astype(BF16)
-        return jnp.concatenate([high, (value - high.astype(F32)).astype(BF16)], axis=0)
-
-    norm = lax.fori_loop(0, 11, norm_step, jnp.zeros((2 * NPROJ, 2 * GROUPS), F32))
-    norm = norm[:NPROJ] + norm[NPROJ:]
-    norm = norm[:, :GROUPS] + norm[:, GROUPS:]
-    grow = lax.broadcasted_iota(jnp.int32, (GROUPS, 128), 0)
-    members = (group_row == grow.astype(F32)).astype(F32)
-    penalty = jnp.dot(norm, members, precision=HIGHEST, preferred_element_type=F32)
-    orient_row = jnp.concatenate([orient_ref[...].astype(F32), jnp.zeros((1, 80), F32)], axis=1)
-    orient_col = jnp.transpose(jnp.broadcast_to(orient_row, (128, 128)))[:NPROJ, :]
-    prior = jnp.zeros((NPROJ, 1), F32)
-    for half in range(2):
-        hit = orient_col == (lane + half * 128).astype(F32)
-        prior += jnp.sum(
-            jnp.where(hit, prior_ref[half : half + 1, :], 0.0), axis=1, keepdims=True
-        )
-    base = prior - penalty
-    span = pl.ds(pl.multiple_of(img * 128, 128), 256)
-    curve = curve_ref[:, span]
-    gain_out[...] = pltpu.roll(curve * curve * noise_row(img, 2), lax.rem(256 - 4 * img, 256), 1)
-
     score[...] = jnp.zeros_like(score)
 
     def process(b, last=False):
@@ -417,6 +383,40 @@
     process_all([shard(y_up, 1), shard(y, 2), shard(y_down, 3), shard(y_up, 3)])
     take_far(1)
     process_all([shard(y_far, 1), shard(y_down, 2), shard(y_up, 2)])
+    def norm_step(t, total):
+        span = pl.ds(pl.multiple_of(t * 384, 128), 384)
+        re = planes[0, :, span].astype(F32)
+        im = planes[1, :, span].astype(F32)
+        curve = curve_ref[:, span]
+        gain = 0.5 * (curve * curve * noise_row(3 * t, 3))
+        power = re * re + im * im
+        return total + lax.dot_general(
+            two_parts(power), two_parts(gain), NT, preferred_element_type=F32
+        )
+
+    def two_parts(value):
+        high = value.astype(BF16)
+        return jnp.concatenate([high, (value - high.astype(F32)).astype(BF16)], axis=0)
+
+    norm = lax.fori_loop(0, 11, norm_step, jnp.zeros((2 * NPROJ, 2 * GROUPS), F32))
+    norm = norm[:NPROJ] + norm[NPROJ:]
+    norm = norm[:, :GROUPS] + norm[:, GROUPS:]
+    grow = lax.broadcasted_iota(jnp.int32, (GROUPS, 128), 0)
+    members = (group_row == grow.astype(F32)).astype(F32)
+    penalty = jnp.dot(norm, members, precision=HIGHEST, preferred_element_type=F32)
+    orient_row = jnp.concatenate([orient_ref[...].astype(F32), jnp.zeros((1, 80), F32)], axis=1)
+    orient_col = jnp.transpose(jnp.broadcast_to(orient_row, (128, 128)))[:NPROJ, :]
+    prior = jnp.zeros((NPROJ, 1), F32)
+    for half in range(2):
+        hit = orient_col == (lane + half * 128).astype(F32)
+        prior += jnp.sum(
+            jnp.where(hit, prior_ref[half : half + 1, :], 0.0), axis=1, keepdims=True
+        )
+    base = prior - penalty
+    span = pl.ds(pl.multiple_of(img * 128, 128), 256)
+    curve = curve_ref[:, span]
+    gain_out[...] = pltpu.roll(curve * curve * noise_row(img, 2), lax.rem(256 - 4 * img, 256), 1)
+
     take_far(3)
     process(shard(y_far, 3))
     full = jnp.concatenate([score[...], jnp.zeros((ROWS, 128 - NPROJ), F32)], axis=1)

time: 61.3 us -> 61.5 us (level); the launches traced: 60.2 us -> 61.1 us
  Pallas kernels: 59.6 us -> 60.4 us
    pallas_call x1, Pallas kernels: 57.8 us -> 58.7 us  [on_device(): pl.pallas_call(body, out_shape=(jax.ShapeDtypeStruct((2, NPROJ, 256), F32...]
where the time goes in v10:
time: 61.5 us; the launch traced here: 61.1 us
  Pallas kernels  60.4 us (98%)
  between operations  0.64 us (1%)
    pallas_call x1, Pallas kernels, on_device(): pl.pallas_call(body, out_shape=(jax.ShapeDtypeStruct((2, NPROJ, 256), F32...  58.7 us
    pallas_call x1, Pallas kernels, on_device(): pl.pallas_call(finish, out_shape=(jax.ShapeDtypeStruct((NPROJ, 2, 132), F...  1.8 us

profile of v10, /device:TPU:1, one launch (start us, length us, event | category | flops | bytes accessed | tf_op | source)
XLA Modules:
  0.0 61.1 jit_solution(14728776990568382979)
XLA Ops:
  0.6 58.7 %expectation.1 = (f32[2,48,256]{2,1,0:T(8,128)}, f32[16,128]{1,0:T(8,128)}, f32[16,256]{1,0:T(8,128)}, f32[1,128]{1,0:T(1,128)}) custom-call(bf16[64,2,264]{2,1,0:T(2,128)(2,1)} %img_hbm.1, bf16[48,2,4224]{2,1,0:T(2,128)(2,1)} %proj_hbm.1, f32[16,4224]{1,0:T(8,128)} %curve_hbm.1, f32[33,128]{1,0:T(8,128)} %bitcast.6, s32[1,64]{1,0:T(1,128)} %bitcast.9, ...), custom_call_target="tpu_custom_call" | custom-call | tf_op jit(solution)/shard_map/expectation/pallas_call | solution.py:746
  59.3 1.8 %finish.1 = (f32[48,2,132]{2,1,0:T(2,128)}, f32[48,132]{1,0:T(8,128)}, f32[1,64]{1,0:T(1,128)}) custom-call(f32[2,48,256]{2,1,0:T(8,128)} %get-tuple-element.10.cls_hbm, f32[16,128]{1,0:T(8,128)} %get-tuple-element.11.group_hbm, f32[16,256]{1,0:T(8,128)} %get-tuple-element.12.gain_hbm, f32[1,128]{1,0:T(1,128)} %get-tuple-element.13.ev_hbm), custom_call_target="tpu_custom_call" | custom-call | tf_op jit(solution)/shard_map/finish/pallas_call | solution.py:822
